TPU v7x, 32 devices: a whole 2x2x4 slice. The times are simulated.
32 devices in a mesh: tm: 4 (over y, x), pts: 8 (over z, core).
Axes of the slice: x: 2, y: 2, z: 4, core: 2. Of those that a mesh axis runs over, the one named last changes fastest.
Arguments:
- codes: bfloat16 [11520, 5120], P('tm', 'pts'), as said below
- scales: float32 [11520], P('tm'), may hold values from 0.005 to 0.015
- weights: float32 [5120], P('pts'), may hold values from 0.5 to 4
- freq_indices: int32 [64], replicated, may hold values from 0 to 127, as said below
Outputs:
- cross_spectral: float32 [64, 2, 89, 89], P('pts')
Inputs may be any that keep to these rules, and one draw needn't show every extreme that they name: `codes`: whole numbers. `freq_indices`: distinct bins.
All inputs are finite; a program needn't handle non-finite values.
Results may differ from a plain program's by a relative error of at most 0.0011.
Values may be sent and summed in bfloat16 or wider, within the bound.
A program may use at most 64 MiB of HBM per device.

v0:
```python
import functools
import math

import jax
import jax.numpy as jnp
from jax import lax
from jax.experimental import pallas as pl
from jax.experimental.pallas import tpu as pltpu
from jax.sharding import PartitionSpec as P

NFFT = 256
HOP = NFFT // 2
HALO = 192
SLOTS = 24
LANES = 128
MESH = pl.DeviceIdType.MESH


def make_tables(freq_indices):
    sample = jnp.arange(NFFT, dtype=jnp.int32)
    phases = freq_indices[:, None] * sample[None, :] % NFFT
    angles = phases.astype(jnp.float32) * (2.0 * math.pi / NFFT)
    hann_window = 0.5 - 0.5 * jnp.cos(sample.astype(jnp.float32) * (2.0 * math.pi / NFFT))
    cosine_table = (0.25 * hann_window[None, :] * jnp.cos(angles)).astype(jnp.bfloat16)
    sine_table = (-0.25 * hann_window[None, :] * jnp.sin(angles)).astype(jnp.bfloat16)
    return (cosine_table, sine_table)


def block_ranges(rows, nt):
    blocks = rows * nt // HOP - 1
    firsts = [-(-t * rows // HOP) for t in range(nt)] + [blocks]
    return [(firsts[t], min(firsts[t + 1], blocks) - firsts[t]) for t in range(nt)]


def kernel(
    nt, nz, chunks, ranges, total_points,
    codes_hbm, scales_ref, weights_ref, table_ref, out_ref,
    codes_ref, vals, stage, send, recv, part, corebuf, summed, zbuf, gath,
    load_s, halo_s, halo_r, tm_s, tm_r, core_s, core_r, z_s, z_r, g_s, g_r,
):
    rows, points = codes_ref.shape
    t = lax.axis_index("tm")
    p = lax.axis_index("pts")
    z = p // 2
    c = p % 2
    partner = p + 1 - 2 * c
    per = 2 * nz
    half = per // 2
    lane_tiles = points // LANES
    groups = SLOTS // 8
    used = max(count for _, count in ranges)
    step = HALO // 2

    ends = [
        min(-(-(HOP // 2 + (8 * g + 7) * HOP + NFFT) // step) * step, rows) for g in range(groups - 1)
    ] + [rows]
    starts = [0] + ends[:-1]
    loads = [
        pltpu.make_async_copy(
            codes_hbm.at[pl.ds(starts[g], ends[g] - starts[g])],
            codes_ref.at[pl.ds(starts[g], ends[g] - starts[g])],
            load_s.at[g],
        )
        for g in range(groups)
    ]
    for load in loads:
        load.start()

    barrier = pltpu.get_barrier_semaphore()
    for d in range(1, nt):
        pl.semaphore_signal(barrier, inc=1, device_id=((t + d) % nt, p), device_id_type=MESH)
    pl.semaphore_signal(barrier, inc=1, device_id=(t, partner), device_id_type=MESH)
    for d in range(1, nz):
        pl.semaphore_signal(barrier, inc=1, device_id=(t, (z + d) % nz * 2 + c), device_id_type=MESH)

    root_weight = jnp.sqrt(weights_ref[...] / total_points)
    tail = vals.shape[0] - rows - HALO
    vals[pl.ds(rows + HALO, tail), :] = jnp.zeros((tail, points), jnp.bfloat16)
    half_rows = table_ref.shape[1] // 2

    def place(i, lane, result):
        at = (i // 8) * 16 + i % 8
        for part_of in range(2):
            stage[lane, pl.ds(at + 8 * part_of, half_rows, stride=2 * SLOTS), :] = result[part_of]

    for lane in range(lane_tiles):
        for spare in range(used, SLOTS):
            place(spare, lane, [jnp.zeros((half_rows, LANES), jnp.float32)] * 2)

    def dequantize(i, carry):
        at = pl.ds(pl.multiple_of(i * step, step), step)
        vals[at, :] = (codes_ref[at, :].astype(jnp.float32) * scales_ref[at, :]).astype(jnp.bfloat16)
        return carry

    halo = pltpu.make_async_remote_copy(
        src_ref=vals.at[pl.ds(0, HALO)],
        dst_ref=vals.at[pl.ds(rows, HALO)],
        send_sem=halo_s, recv_sem=halo_r,
        device_id=((t + nt - 1) % nt, p), device_id_type=MESH,
    )
    offset = (t % 2) * (HOP // 2)

    def spectra(k, first, last):
        table = table_ref[k]

        def spectrum(i, carry):
            window = vals[pl.ds(pl.multiple_of(offset + i * HOP, HOP // 2), NFFT), :]
            result = jnp.dot(table, window, preferred_element_type=jnp.float32) * root_weight
            for lane in range(lane_tiles):
                columns = result[:, lane * LANES:(lane + 1) * LANES]
                place(i, lane, [columns[:half_rows], columns[half_rows:]])
            return carry

        lax.fori_loop(first, last, spectrum, 0)

    def pack_group(k, g, d):
        dest = (t + d) % nt

        def pack(f, carry):
            base = pl.multiple_of((dest * per + f) * 2 * SLOTS + g * 16, 16)
            for lane in range(lane_tiles):
                block = stage[lane, pl.ds(base, 16), :].astype(jnp.bfloat16)
                at = slice(lane * LANES, (lane + 1) * LANES)
                if d == 0:
                    recv[k, f, t, g * 16:(g + 1) * 16, at] = block
                else:
                    send[k, d - 1, f, g * 16:(g + 1) * 16, at] = block
            return carry

        lax.fori_loop(0, per, pack, 0)

    def exchange(k, piece, d):
        if k < chunks - 1:
            src = send.at[k, d - 1, :, pl.ds(piece * 16, 16)]
            dst = recv.at[k, :, t, pl.ds(piece * 16, 16)]
        else:
            src = send.at[k, d - 1, pl.ds(piece * half, half)]
            dst = recv.at[k, pl.ds(piece * half, half), t]
        return pltpu.make_async_remote_copy(
            src_ref=src, dst_ref=dst,
            send_sem=tm_s.at[k, piece, d - 1], recv_sem=tm_r.at[k, piece, d - 1],
            device_id=((t + d) % nt, p), device_id_type=MESH,
        )

    safe = (rows - HOP // 2 - NFFT) // HOP + 1
    partners = (3, 1, 2)
    for k in range(chunks):
        for g in range(groups):
            first, last = 8 * g, min(8 * g + 8, used)
            if k == 0:
                loads[g].wait()
                lax.fori_loop(starts[g] // step, ends[g] // step, dequantize, 0)
                if g == 0:
                    pl.semaphore_wait(barrier, nt + nz - 1)
                    halo.start()
                if last > safe:
                    spectra(k, first, safe)
                    halo.wait()
                    first = safe
            spectra(k, first, last)
            for d in partners + (0,):
                pack_group(k, g, d)
                if d and k < chunks - 1:
                    exchange(k, g, d).start()
        if k == chunks - 1:
            for h in range(2):
                for d in partners:
                    exchange(k, h, d).start()

    width = nt * 2 * SLOTS
    wide = 2 * LANES
    eights = nt * groups
    lane_in = lax.broadcasted_iota(jnp.int32, (1, wide), 1) % 16 < 8
    sign = jnp.where(lane_in, -1.0, 1.0)

    def to_core(k, h):
        at = pl.ds(h * nz // 2, nz // 2)
        return pltpu.make_async_remote_copy(
            src_ref=part.at[k, at, 1 - c], dst_ref=corebuf.at[k, at],
            send_sem=core_s.at[k, h], recv_sem=core_r.at[k, h],
            device_id=(t, partner), device_id_type=MESH,
        )

    def to_z(k, peer):
        return pltpu.make_async_remote_copy(
            src_ref=summed.at[k, peer], dst_ref=zbuf.at[k, z],
            send_sem=z_s.at[k, peer], recv_sem=z_r.at[k, z],
            device_id=(t, peer * 2 + c), device_id_type=MESH,
        )

    def from_z(k, peer):
        return pltpu.make_async_remote_copy(
            src_ref=summed.at[k, peer], dst_ref=zbuf.at[k, peer],
            send_sem=z_s.at[k, peer], recv_sem=z_r.at[k, peer],
            device_id=(t, peer * 2 + c), device_id_type=MESH,
        )

    def to_tm(k, d):
        return pltpu.make_async_remote_copy(
            src_ref=gath.at[t, k], dst_ref=gath.at[t, k],
            send_sem=g_s.at[k, d - 1], recv_sem=g_r.at[k, d - 1],
            device_id=((t + d) % nt, p), device_id_type=MESH,
        )

    def cross_half(k, h):
        def cross(f, carry):
            stacked = recv[k, f].reshape(width, points)
            prod = lax.dot_general(
                stacked, stacked, (((1,), (1,)), ((), ())), preferred_element_type=jnp.float32
            )
            real = jnp.concatenate([prod[16 * m:16 * m + 8] for m in range(eights)], axis=0)
            imag = jnp.concatenate([prod[16 * m + 8:16 * m + 16] for m in range(eights)], axis=0)
            fill = jnp.zeros((nt * SLOTS, wide - width), jnp.float32)
            real = jnp.concatenate([real, fill], axis=1)
            imag = jnp.concatenate([imag, fill], axis=1)
            both = real + sign * imag
            both = both + pltpu.roll(both, wide - 8, 1)
            moved = pltpu.roll(both, wide - (LANES - 8), 1)
            part[k, f // 2, f % 2] = jnp.where(lane_in[:, :LANES], both[:, :LANES], moved[:, :LANES])
            return carry

        lax.fori_loop(h * half, (h + 1) * half, cross, 0)
        to_core(k, h).start()
        to_core(k, h).wait()
        for peer in range(h * nz // 2, (h + 1) * nz // 2):
            summed[k, peer] = part[k, peer, c] + corebuf[k, peer]

            @pl.when(peer != z)
            def _():
                to_z(k, peer).start()

    def compress(padded):
        kept = [padded[s * SLOTS:s * SLOTS + ranges[s][1]] for s in range(nt)]
        fill = LANES - sum(n for _, n in ranges)
        return jnp.concatenate(kept + [jnp.zeros((fill, LANES), jnp.float32)], axis=0)

    def reduce_z(k):
        total = summed[k, z]
        for d in range(1, nz):
            peer = (z + d) % nz
            from_z(k, peer).wait()
            total = total + zbuf[k, peer]
        full = jnp.concatenate([total, jnp.zeros((LANES - nt * SLOTS, LANES), jnp.float32)], axis=0)
        turned = full.T
        where = [16 * m if m < 8 else 16 * (m - 8) + 8 for m in range(eights)]
        turned = jnp.concatenate([turned[w:w + 8] for w in where], axis=0)
        gath[t, k] = compress(compress(turned).T)[:nt * SLOTS]
        for d in range(1, nt):
            to_tm(k, d).start()

    def finish(k):
        for d in range(1, nt):
            to_tm(k, d).wait()

        def one(s, carry):
            ordered = gath[s, k]
            fill = jnp.zeros((LANES - nt * SLOTS, LANES), jnp.float32)
            mirrored = jnp.concatenate([ordered, fill], axis=0).T[:nt * SLOTS]
            out_ref[s * chunks + k, 0] = 0.5 * (ordered + mirrored)
            out_ref[s * chunks + k, 1] = 0.5 * (ordered - mirrored)
            return carry

        lax.fori_loop(0, nt, one, 0)

    for k in range(chunks):
        for h in range(2):
            if k == chunks - 1:
                for d in partners:
                    exchange(k, h, d).wait()
            elif h == 0:
                for g in range(groups):
                    for d in partners:
                        exchange(k, g, d).wait()
            cross_half(k, h)
        if k < chunks - 1:
            reduce_z(k)
    for k in range(chunks - 1):
        finish(k)
    reduce_z(chunks - 1)
    finish(chunks - 1)


def fused(nt, np_, codes, scales, weights, freq_indices):
    rows, points = codes.shape
    nf = freq_indices.shape[0]
    nz = np_ // 2
    chunks = nf // (nt * np_)
    ranges = block_ranges(rows, nt)
    blocks = rows * nt // HOP - 1
    order = freq_indices.reshape(np_, nt, chunks).transpose(2, 1, 0).reshape(-1)
    cosine_table, sine_table = make_tables(order)
    shape = (chunks, nt * np_, NFFT)
    table = jnp.concatenate([cosine_table.reshape(shape), sine_table.reshape(shape)], axis=1)
    height = nt * SLOTS
    used = max(count for _, count in ranges)
    vals_rows = HOP // 2 + (used - 1) * HOP + NFFT
    groups = SLOTS // 8
    f32, bf16 = jnp.float32, jnp.bfloat16
    dma = pltpu.SemaphoreType.DMA
    vmem = pl.BlockSpec(memory_space=pltpu.VMEM)
    full = pl.pallas_call(
        functools.partial(kernel, nt, nz, chunks, ranges, points * np_),
        out_shape=jax.ShapeDtypeStruct((nt * chunks, 2, height, LANES), f32),
        in_specs=[pl.BlockSpec(memory_space=pl.ANY)] + [vmem] * 3,
        out_specs=vmem,
        scratch_shapes=[
            pltpu.VMEM((rows, points), bf16),
            pltpu.VMEM((vals_rows, points), bf16),
            pltpu.VMEM((points // LANES, nt * np_ * 2 * SLOTS, LANES), f32),
            pltpu.VMEM((chunks, nt - 1, np_, 2 * SLOTS, points), bf16),
            pltpu.VMEM((chunks, np_, nt, 2 * SLOTS, points), bf16),
            pltpu.VMEM((chunks, nz, 2, height, LANES), f32),
            pltpu.VMEM((chunks, nz, height, LANES), f32),
            pltpu.VMEM((chunks, nz, height, LANES), f32),
            pltpu.VMEM((chunks, nz, height, LANES), f32),
            pltpu.VMEM((nt, chunks, height, LANES), f32),
            dma((groups,)),
            dma, dma,
            dma((chunks, groups, nt - 1)), dma((chunks, groups, nt - 1)),
            dma((chunks, 2)), dma((chunks, 2)),
            dma((chunks, nz)), dma((chunks, nz)),
            dma((chunks, nt - 1)), dma((chunks, nt - 1)),
        ],
        compiler_params=pltpu.CompilerParams(
            collective_id=0, has_side_effects=True, vmem_limit_bytes=52 * 2**20
        ),
        name="spectra_cross",
    )(codes, scales.reshape(-1, 1), weights.reshape(1, -1), table)
    return full[:, :, :blocks, :blocks]


def cross_matrices(stacked):
    blocks = stacked.shape[1] // 2
    products = jnp.einsum("fip,fjp->fij", stacked, stacked, preferred_element_type=jnp.float32)
    matrix_re = products[:, :blocks, :blocks] + products[:, blocks:, blocks:]
    matrix_im = products[:, :blocks, blocks:] - products[:, blocks:, :blocks]
    return jnp.stack([matrix_re, matrix_im], axis=1)


def general(codes, scales, weights, freq_indices):
    values = (codes.astype(jnp.float32) * scales[:, None]).astype(jnp.bfloat16)
    regrouped = lax.all_to_all(values, "tm", split_axis=1, concat_axis=0, tiled=True)
    point_count = regrouped.shape[1]
    own_weights = lax.dynamic_slice_in_dim(
        weights, lax.axis_index("tm") * point_count, point_count, 0
    )
    total_points = weights.shape[0] * lax.axis_size("pts")
    root_weight = jnp.sqrt(own_weights / total_points)
    cosine_table, sine_table = make_tables(freq_indices)
    hop_rows = regrouped.reshape(-1, NFFT // 2, point_count)
    windows = jnp.concatenate([hop_rows[:-1], hop_rows[1:]], axis=1)
    real_part = jnp.einsum("fn,bnp->fbp", cosine_table, windows, preferred_element_type=jnp.float32)
    imag_part = jnp.einsum("fn,bnp->fbp", sine_table, windows, preferred_element_type=jnp.float32)
    scaled_re = (real_part * root_weight[None, None, :]).astype(jnp.bfloat16)
    scaled_im = (imag_part * root_weight[None, None, :]).astype(jnp.bfloat16)
    stacked = jnp.concatenate([scaled_re, scaled_im], axis=1)
    partial_value = lax.psum_scatter(
        cross_matrices(stacked), "pts", scatter_dimension=0, tiled=True
    )
    return lax.psum(partial_value, "tm")


def solution(mesh):
    nt, np_ = mesh.shape["tm"], mesh.shape["pts"]

    def per_device(codes, scales, weights, freq_indices):
        rows, points = codes.shape
        fits = (
            nt == 4
            and np_ == 8
            and freq_indices.shape[0] % (nt * np_) == 0
            and points % LANES == 0
            and rows % HALO == 0
            and rows % HOP == HOP // 2
            and max(count for _, count in block_ranges(rows, nt)) <= SLOTS
        )
        if fits:
            return fused(nt, np_, codes, scales, weights, freq_indices)
        return general(codes, scales, weights, freq_indices)

    return jax.shard_map(
        per_device,
        mesh=mesh,
        in_specs=(P("tm", "pts"), P("tm"), P("pts"), P()),
        out_specs=P("pts", None, None, None),
        check_vma=False,
    )
```

profile of v0, /device:TPU:8, one launch (start us, length us, event | category | flops | bytes accessed | tf_op | source)
XLA Modules:
  0.0 73.4 jit_solution(2303316703689081435)
XLA Ops:
  0.0 0.7 reshape.53.weights_ref
  0.7 0.8 %reshape.54 = s32[8,4,2]{2,1,0:T(4,128)S(1)} reshape(s32[64]{0:T(128)} %param.7) | data formatting | bytes 512 | tf_op jit(solution)/shard_map/reshape | solution.py:290
  1.5 0.1 copy.7
  1.6 0.1 mul.98
  1.7 0.4 multiply_convert_fusion.1
  2.1 2.3 %reshape.55.scales_ref = f32[2880,1]{1,0:T(8,128)} reshape(f32[2880]{0:T(1024)} %param.5) | data formatting | bytes 23040 | tf_op jit(solution)/shard_map/reshape | solution.py:328
  4.4 67.6 %spectra_cross.1 = f32[8,2,96,128]{3,2,1,0:T(8,128)S(1)} custom-call(bf16[2880,640]{1,0:T(8,128)(2,1)} %codes_hbm.1, f32[2880,1]{1,0:T(8,128)} %reshape.55.scales_ref, f32[1,640]{1,0:T(1,128)S(1)} %reshape.53.weights_ref, bf16[2,64,256]{2,1,0:T(8,128)(2,1)S(1)} %pad_maximum_fusion.table_ref), custom_call_target="tpu_custom_call" | custom-call | tf_op jit(solution)/shard_map/spectra_cross/pallas_call | solution.py:301
  71.9 1.4 %copy.9 = f32[8,2,89,89]{3,1,2,0:T(2,128)} copy(f32[8,2,89,89]{3,2,1,0:T(8,128)S(1)} %bitcast.2) | data formatting | bytes 1013888 | tf_op jit(solution)/shard_map/slice | solution.py:329
  (2 shorter events, 0.1 us)
where the time goes:
time: 74.4 us; the launch traced here: 73.4 us
  Pallas kernels  67.6 us (91%)
  local copies, waits for them, and re-layouts  5.36 us (7%)
    pallas_call x1, Pallas kernels, fused(): pl.pallas_call(functools.partial(kernel, nt, nz, chunks, ranges, points *...  67.6 us
    reshape x1, local copies, waits for them, and re-layouts, fused(): scales.reshape(-1, 1)  2.29 us

commit v1 on v0

v1 whole, which is shorter than its diff:
```python
import functools
import math

import jax
import jax.numpy as jnp
from jax import lax
from jax.experimental import pallas as pl
from jax.experimental.pallas import tpu as pltpu
from jax.sharding import PartitionSpec as P

NFFT = 256
HOP = NFFT // 2
HALF = HOP // 2
LANES = 128
SLOTS = 96
NT = 4
NZ = 4
QUARTERS = 4
ZSETS = ((0, 3), (1, 2))
MESH = pl.DeviceIdType.MESH


def make_tables(freq_indices):
    sample = jnp.arange(NFFT, dtype=jnp.int32)
    phases = freq_indices[:, None] * sample[None, :] % NFFT
    angles = phases.astype(jnp.float32) * (2.0 * math.pi / NFFT)
    hann_window = 0.5 - 0.5 * jnp.cos(sample.astype(jnp.float32) * (2.0 * math.pi / NFFT))
    cosine_table = (0.25 * hann_window[None, :] * jnp.cos(angles)).astype(jnp.bfloat16)
    sine_table = (-0.25 * hann_window[None, :] * jnp.sin(angles)).astype(jnp.bfloat16)
    return (cosine_table, sine_table)


def turn_cosine(turn):
    left = 64 - jnp.minimum(turn, NFFT - turn)
    x = left.astype(jnp.float32) * (2.0 * math.pi / NFFT)
    y = x * x
    poly = jnp.full_like(x, -1.0 / 39916800.0)
    for c in (1.0 / 362880.0, -1.0 / 5040.0, 1.0 / 120.0, -1.0 / 6.0, 1.0):
        poly = poly * y + c
    return x * poly


def kernel(
    total_points,
    codes_hbm, scales_hbm, weights_hbm, freq_ref, out_ref,
    codes_ref, scales_v, weights_v, spread, vals, table, sbuf, rbuf, spbuf, sprecv, stage,
    part, corebuf, summed, zbuf, gath,
    load_s, halo_s, halo_r, tm_s, tm_r, sp_s, sp_r, core_s, core_r, z_s, z_r, g_s, g_r,
):
    rows, points = codes_ref.shape
    t = lax.axis_index("tm")
    p = lax.axis_index("pts")
    z = p // 2
    c = p % 2
    odd = t % 2
    partner = p + 1 - 2 * c
    lane_tiles = points // LANES
    blocks = rows // HOP
    pairs = blocks // 2
    padded = rows + HALF

    early = (10 * HOP)
    late = rows - early - HALF
    edge_at = (1 - odd) * (rows - HALF)
    early_at = odd * (rows - early)
    late_at = odd * HALF + (1 - odd) * early

    def load(at, count, sem):
        at = pl.ds(pl.multiple_of(at, HALF), count)
        return pltpu.make_async_copy(codes_hbm.at[at], codes_ref.at[at], load_s.at[sem])

    load_scales = pltpu.make_async_copy(scales_hbm, scales_v, load_s.at[3])
    load_weights = pltpu.make_async_copy(weights_hbm, weights_v, load_s.at[4])
    load_edge = load(edge_at, HALF, 0)
    load_early = load(early_at, early, 1)
    load_late = load(late_at, late, 2)
    barrier = pltpu.get_barrier_semaphore()
    for d in range(1, NT):
        pl.semaphore_signal(barrier, inc=1, device_id=(t ^ d, p), device_id_type=MESH)
    pl.semaphore_signal(barrier, inc=1, device_id=(t, partner), device_id_type=MESH)
    for d in range(1, NZ):
        pl.semaphore_signal(barrier, inc=1, device_id=(t, (z + d) % NZ * 2 + c), device_id_type=MESH)
    load_scales.start()
    load_edge.start()
    load_early.start()
    load_weights.start()
    load_late.start()

    sample = lax.broadcasted_iota(jnp.int32, (8, NFFT), 1)
    sub = lax.broadcasted_iota(jnp.int32, (8, NFFT), 0)
    window_shape = 0.25 * (0.5 - 0.5 * turn_cosine(sample))
    shift = (sub % 2) * (NFFT // 4)

    def octet_table(dest, q):
        bins = jnp.zeros((8, NFFT), jnp.int32)
        for j in range(4):
            dest_p = ZSETS[q % 2][j // 2] * 2 + j % 2
            bins = jnp.where(sub // 2 == j, freq_ref[dest_p * 2 * NT + dest * 2 + q // 2], bins)
        return window_shape * turn_cosine((bins * sample + shift) % NFFT)

    for dest in range(NT):
        for half in range(2):
            at = dest * 32 + half * 16
            pair = [octet_table(dest, 2 * half), octet_table(dest, 2 * half + 1)]
            table[at:at + 16, :] = jnp.concatenate(pair, axis=0).astype(jnp.bfloat16)

    load_scales.wait()
    for g in range(-(-rows // HOP)):
        count = min(HOP, rows - g * HOP)
        line = scales_v[g * HOP:g * HOP + count].reshape(1, count)
        spread[g * HOP:g * HOP + count, :] = jnp.broadcast_to(line, (LANES, count)).T

    offset = odd * HALF

    def dequantize(i, carry):
        at = pl.ds(pl.multiple_of(i * HALF, HALF), HALF)
        to = pl.ds(pl.multiple_of(i * HALF + offset, HALF), HALF)
        scale = spread[at, :]
        for lane in range(lane_tiles):
            cols = slice(lane * LANES, (lane + 1) * LANES)
            vals[to, cols] = (codes_ref[at, cols].astype(jnp.float32) * scale).astype(jnp.bfloat16)
        return carry

    load_edge.wait()
    dequantize(edge_at // HALF, 0)
    halo_from = (1 - odd) * (rows - HALF) + odd * HALF
    halo_to = odd * rows
    halo_mine = (1 - odd) * rows

    def halo_copy(dst):
        return pltpu.make_async_remote_copy(
            src_ref=vals.at[pl.ds(pl.multiple_of(halo_from, HALF), HALF)],
            dst_ref=vals.at[pl.ds(pl.multiple_of(dst, HALF), HALF)],
            send_sem=halo_s, recv_sem=halo_r,
            device_id=(t ^ 1, p), device_id_type=MESH,
        )

    pl.semaphore_wait(barrier, NT + NZ - 1)
    halo_copy(halo_to).start()

    load_early.wait()
    lax.fori_loop(early_at // HALF, (early_at + early) // HALF, dequantize, 0)
    load_weights.wait()
    root_weight = jnp.sqrt(weights_v[...].reshape(1, points) / total_points)

    def spectrum(i):
        window = vals[pl.ds(pl.multiple_of(i * HOP, HOP), NFFT), :]
        return jnp.dot(table[...], window, preferred_element_type=jnp.float32) * root_weight

    def spectra(j, carry):
        jj = odd * (pairs - 1 - j) + (1 - odd) * j
        first = spectrum(2 * jj)
        second = spectrum(2 * jj + 1)
        for dest in range(NT):
            for q in range(QUARTERS):
                at = slice(dest * 32 + q * 8, dest * 32 + q * 8 + 8)
                both = jnp.concatenate([first[at], second[at]], axis=0)
                sbuf[q, dest, jj] = both.astype(jnp.bfloat16)
        return carry

    cuts = (0, 4, pairs - 1, pairs)
    partners = (3, 1, 2)

    def tiles_of(who, piece):
        count = cuts[piece + 1] - cuts[piece]
        flip = who % 2
        return flip * (pairs - cuts[piece + 1]) + (1 - flip) * cuts[piece], count

    def exchange(q, piece, d, source):
        at, count = tiles_of(source, piece)
        return pltpu.make_async_remote_copy(
            src_ref=sbuf.at[q, t ^ d, pl.ds(at, count)],
            dst_ref=rbuf.at[q, source, pl.ds(at, count)],
            send_sem=tm_s.at[q, piece, d - 1], recv_sem=tm_r.at[q, piece, d - 1],
            device_id=(t ^ d, p), device_id_type=MESH,
        )

    def straddle(h, d, source):
        return pltpu.make_async_remote_copy(
            src_ref=spbuf.at[h, t ^ d],
            dst_ref=sprecv.at[h, source - 1],
            send_sem=sp_s.at[h, d - 1], recv_sem=sp_r.at[h, d - 1],
            device_id=(t ^ d, p), device_id_type=MESH,
        )

    middle = (t == 1) | (t == 2)

    def send_straddle(h):
        @pl.when(middle)
        def _():
            for d in partners:
                straddle(h, d, t).start()

    def send(q, piece):
        for d in partners:
            exchange(q, piece, d, t).start()

    lax.fori_loop(cuts[0], cuts[1], spectra, 0)
    send(0, 0)
    load_late.wait()
    lax.fori_loop(late_at // HALF, (late_at + late) // HALF, dequantize, 0)
    lax.fori_loop(cuts[1], cuts[2], spectra, 0)
    send(0, 1)
    halo_copy(halo_mine).wait_recv()
    lax.fori_loop(cuts[2], cuts[3], spectra, 0)
    send(0, 2)

    @pl.when(middle)
    def _():
        hop = pl.ds(pl.multiple_of(odd * (padded - HOP), HOP), HOP)
        side = jnp.where(odd == 1, table[:, :HOP].astype(jnp.float32), table[:, HOP:].astype(jnp.float32))
        result = jnp.dot(side.astype(jnp.bfloat16), vals[hop, :], preferred_element_type=jnp.float32)
        result = (result * root_weight).astype(jnp.bfloat16)
        for dest in range(NT):
            for h in range(2):
                spbuf[h, dest] = result[dest * 32 + h * 16:dest * 32 + h * 16 + 16]
        for h in range(2):
            sprecv[h, t - 1] = spbuf[h, t]

    for h in range(2):
        send_straddle(h)
    for piece in range(3):
        send(1, piece)

    for lane in range(lane_tiles):
        for s in range(8):
            stage[lane, s * SLOTS + SLOTS - 8:(s + 1) * SLOTS, :] = jnp.zeros((8, LANES), jnp.float32)

    def place(b, octet):
        for lane in range(lane_tiles):
            stage[lane, pl.ds(b, 8, stride=SLOTS), :] = octet[:, lane * LANES:(lane + 1) * LANES]

    def unpack(source_ref, q, who, piece):
        at, count = tiles_of(who, piece)
        base = who * blocks + who // 2

        def one(i, carry):
            tile = source_ref[q, who, i].astype(jnp.float32)
            place(base + 2 * i, tile[:8])
            place(base + 2 * i + 1, tile[8:])
            return carry

        lax.fori_loop(at, at + count, one, 0)

    def gram(q, j):
        at = slice(j * 2 * SLOTS, (j + 1) * 2 * SLOTS)
        stacked = jnp.concatenate(
            [stage[lane, at, :].astype(jnp.bfloat16) for lane in range(lane_tiles)], axis=1
        )
        fill = jnp.zeros((LANES - SLOTS, points), jnp.bfloat16)
        wide = jnp.concatenate([stacked[:SLOTS], fill, stacked[SLOTS:], fill], axis=0)
        prod = lax.dot_general(
            stacked, wide, (((1,), (1,)), ((), ())), preferred_element_type=jnp.float32
        )
        real = prod[:SLOTS, :LANES] + prod[SLOTS:, LANES:]
        imag = prod[:SLOTS, LANES:] - prod[SLOTS:, :LANES]
        part[q, j % 2, j // 2] = real + imag

    def to_core(q):
        return pltpu.make_async_remote_copy(
            src_ref=part.at[q, 1 - c], dst_ref=corebuf.at[q],
            send_sem=core_s.at[q], recv_sem=core_r.at[q],
            device_id=(t, partner), device_id_type=MESH,
        )

    def to_z(q, s, source):
        return pltpu.make_async_remote_copy(
            src_ref=summed.at[q, s], dst_ref=zbuf.at[q, source],
            send_sem=z_s.at[q, s], recv_sem=z_r.at[q, source],
            device_id=(t, ZSETS[q % 2][s] * 2 + c), device_id_type=MESH,
        )

    def to_tm(k, d, source):
        return pltpu.make_async_remote_copy(
            src_ref=gath.at[source, k], dst_ref=gath.at[source, k],
            send_sem=g_s.at[k, d - 1], recv_sem=g_r.at[k, d - 1],
            device_id=(t ^ d, p), device_id_type=MESH,
        )

    def receive(q):
        for piece in range(3):
            unpack(sbuf, q, t, piece)
        for piece in range(3):
            for d in partners:
                exchange(q, piece, d, t ^ d).wait_recv()
                unpack(rbuf, q, t ^ d, piece)
        h = q // 2
        if q % 2 == 0:
            for d in partners:
                source = t ^ d

                @pl.when((source == 1) | (source == 2))
                def _():
                    straddle(h, d, source).wait_recv()
        both = sprecv[h, 0].astype(jnp.float32) + sprecv[h, 1].astype(jnp.float32)
        at = q % 2 * 8
        place(2 * blocks, both[at:at + 8])

    def core_stage(q):
        to_core(q).wait()
        for s in range(2):
            summed[q, s] = part[q, c, s] + corebuf[q, s]

            @pl.when(z != ZSETS[q % 2][s])
            def _():
                to_z(q, s, z).start()

    def z_stage(q):
        for s in range(2):
            home = ZSETS[q % 2][s]

            @pl.when(z == home)
            def _():
                total = summed[q, s]
                for other in range(NZ):
                    if other != home:
                        to_z(q, s, other).wait_recv()
                        total = total + zbuf[q, other]
                gath[t, q // 2] = total
                for d in partners:
                    to_tm(q // 2, d, t).start()

    def finish(k):
        for d in partners:
            to_tm(k, d, t ^ d).wait_recv()

        def one(s, carry):
            ordered = gath[s, k]
            fill = jnp.zeros((LANES - SLOTS, LANES), jnp.float32)
            mirrored = jnp.concatenate([ordered, fill], axis=0).T[:SLOTS]
            out_ref[s * 2 + k, 0] = 0.5 * (ordered + mirrored)
            out_ref[s * 2 + k, 1] = 0.5 * (ordered - mirrored)
            return carry

        lax.fori_loop(0, NT, one, 0)

    for q in range(QUARTERS):
        if 0 < q < QUARTERS - 1:
            for piece in range(3):
                send(q + 1, piece)
        receive(q)
        for j in (0, 2, 1, 3):
            gram(q, j)
        to_core(q).start()
        if q >= 1:
            z_stage(q - 1)
        core_stage(q)
    z_stage(QUARTERS - 1)
    finish(0)
    finish(1)

    halo_copy(halo_to).wait_send()
    for q in range(QUARTERS):
        for piece in range(3):
            for d in partners:
                exchange(q, piece, d, t).wait_send()
        for s in range(2):
            @pl.when(z != ZSETS[q % 2][s])
            def _():
                to_z(q, s, z).wait_send()
    for k in range(2):
        for d in partners:
            to_tm(k, d, t).wait_send()

    @pl.when(middle)
    def _():
        for h in range(2):
            for d in partners:
                straddle(h, d, t).wait_send()


def fused(codes, scales, weights, freq_indices, total_points):
    rows, points = codes.shape
    blocks = rows // HOP
    pairs = blocks // 2
    f32, bf16 = jnp.float32, jnp.bfloat16
    dma = pltpu.SemaphoreType.DMA
    hbm = pl.BlockSpec(memory_space=pl.ANY)
    full = pl.pallas_call(
        functools.partial(kernel, total_points),
        out_shape=jax.ShapeDtypeStruct((2 * NT, 2, SLOTS, LANES), f32),
        in_specs=[hbm, hbm, hbm, pl.BlockSpec(memory_space=pltpu.SMEM)],
        out_specs=pl.BlockSpec(memory_space=pltpu.VMEM),
        scratch_shapes=[
            pltpu.VMEM((rows, points), bf16),
            pltpu.VMEM((rows,), f32),
            pltpu.VMEM((points,), f32),
            pltpu.VMEM((rows, LANES), f32),
            pltpu.VMEM((rows + HALF, points), bf16),
            pltpu.VMEM((2 * NT * QUARTERS * 4, NFFT), bf16),
            pltpu.VMEM((QUARTERS, NT, pairs, 16, points), bf16),
            pltpu.VMEM((QUARTERS, NT, pairs, 16, points), bf16),
            pltpu.VMEM((2, NT, 16, points), bf16),
            pltpu.VMEM((2, 2, 16, points), bf16),
            pltpu.VMEM((points // LANES, 8 * SLOTS, LANES), f32),
            pltpu.VMEM((QUARTERS, 2, 2, SLOTS, LANES), f32),
            pltpu.VMEM((QUARTERS, 2, SLOTS, LANES), f32),
            pltpu.VMEM((QUARTERS, 2, SLOTS, LANES), f32),
            pltpu.VMEM((QUARTERS, NZ, SLOTS, LANES), f32),
            pltpu.VMEM((NT, 2, SLOTS, LANES), f32),
            dma((5,)),
            dma, dma,
            dma((QUARTERS, 3, NT - 1)), dma((QUARTERS, 3, NT - 1)),
            dma((2, NT - 1)), dma((2, NT - 1)),
            dma((QUARTERS,)), dma((QUARTERS,)),
            dma((QUARTERS, 2)), dma((QUARTERS, NZ)),
            dma((2, NT - 1)), dma((2, NT - 1)),
        ],
        compiler_params=pltpu.CompilerParams(
            collective_id=0, has_side_effects=True, vmem_limit_bytes=52 * 2**20
        ),
        name="spectra_cross",
    )(codes, scales, weights, freq_indices)
    count = rows * NT // HOP - 1
    return full[:, :, :count, :count]


def cross_matrices(stacked):
    blocks = stacked.shape[1] // 2
    products = jnp.einsum("fip,fjp->fij", stacked, stacked, preferred_element_type=jnp.float32)
    matrix_re = products[:, :blocks, :blocks] + products[:, blocks:, blocks:]
    matrix_im = products[:, :blocks, blocks:] - products[:, blocks:, :blocks]
    return jnp.stack([matrix_re, matrix_im], axis=1)


def general(codes, scales, weights, freq_indices):
    values = (codes.astype(jnp.float32) * scales[:, None]).astype(jnp.bfloat16)
    regrouped = lax.all_to_all(values, "tm", split_axis=1, concat_axis=0, tiled=True)
    point_count = regrouped.shape[1]
    own_weights = lax.dynamic_slice_in_dim(
        weights, lax.axis_index("tm") * point_count, point_count, 0
    )
    total_points = weights.shape[0] * lax.axis_size("pts")
    root_weight = jnp.sqrt(own_weights / total_points)
    cosine_table, sine_table = make_tables(freq_indices)
    hop_rows = regrouped.reshape(-1, NFFT // 2, point_count)
    windows = jnp.concatenate([hop_rows[:-1], hop_rows[1:]], axis=1)
    real_part = jnp.einsum("fn,bnp->fbp", cosine_table, windows, preferred_element_type=jnp.float32)
    imag_part = jnp.einsum("fn,bnp->fbp", sine_table, windows, preferred_element_type=jnp.float32)
    scaled_re = (real_part * root_weight[None, None, :]).astype(jnp.bfloat16)
    scaled_im = (imag_part * root_weight[None, None, :]).astype(jnp.bfloat16)
    stacked = jnp.concatenate([scaled_re, scaled_im], axis=1)
    partial_value = lax.psum_scatter(
        cross_matrices(stacked), "pts", scatter_dimension=0, tiled=True
    )
    return lax.psum(partial_value, "tm")


def solution(mesh):
    nt, np_ = mesh.shape["tm"], mesh.shape["pts"]

    def per_device(codes, scales, weights, freq_indices):
        rows, points = codes.shape
        fits = (
            nt == NT
            and np_ == 2 * NZ
            and freq_indices.shape[0] == 2 * nt * np_
            and points % LANES == 0
            and rows % NFFT == HALF
            and rows >= 16 * HOP
            and 4 * (rows // HOP) + 1 <= SLOTS
        )
        if fits:
            return fused(codes, scales, weights, freq_indices, points * np_)
        return general(codes, scales, weights, freq_indices)

    return jax.shard_map(
        per_device,
        mesh=mesh,
        in_specs=(P("tm", "pts"), P("tm"), P("pts"), P()),
        out_specs=P("pts", None, None, None),
        check_vma=False,
    )
```

time: 74.4 us -> 65.3 us (0.88)
  Pallas kernels: 67.6 us -> 60.8 us
  local copies, waits for them, and re-layouts: 5.36 us -> 3.47 us
    pallas_call x1, Pallas kernels: 67.6 us -> 60.8 us  [fused(): pl.pallas_call(functools.partial(kernel, total_points), out_shape=jax.Sha...]
    reshape x3 -> x0, local copies, waits for them, and re-layouts: 3.75 us -> none  [the longest x1 2.29 us: fused(): scales.reshape(-1, 1)]
    unnamed x0 -> x6, local copies, waits for them, and re-layouts: none -> 2.05 us
where the time goes in v1:
time: 65.3 us; the launch traced here: 64.3 us
  Pallas kernels  60.8 us (93%)
  local copies, waits for them, and re-layouts  3.47 us (5%)
    pallas_call x1, Pallas kernels, fused(): pl.pallas_call(functools.partial(kernel, total_points), out_shape=jax.Sha...  60.8 us
    unnamed x6, local copies, waits for them, and re-layouts  2.05 us
    slice x1, local copies, waits for them, and re-layouts, fused(): return full[:, :, :count, :count]  1.43 us

profile of v1, /device:TPU:8, one launch (start us, length us, event | category | flops | bytes accessed | tf_op | source)
XLA Modules:
  0.0 64.3 jit_solution(2977167856769157694)
XLA Ops:
  0.0 0.0 copy-start
  0.0 0.7 %copy-done = f32[2880]{0:T(1024)S(1)} copy-done((f32[2880]{0:T(1024)S(1)}, f32[2880]{0:T(1024)}, u32[]{:S(2)}) %copy-start) | copy-done | bytes 11544
  0.7 0.0 copy-start.1
  0.7 0.7 %copy-done.1 = f32[640]{0:T(1024)S(1)} copy-done((f32[640]{0:T(1024)S(1)}, f32[640]{0:T(1024)}, u32[]{:S(2)}) %copy-start.1) | copy-done | bytes 2584
  1.4 0.0 copy-start.2
  1.4 0.7 %copy-done.2 = s32[64]{0:T(128)S(1)} copy-done((s32[64]{0:T(128)S(1)}, s32[64]{0:T(128)}, u32[]{:S(2)}) %copy-start.2) | copy-done | bytes 280
  2.1 60.8 %spectra_cross.1 = f32[8,2,96,128]{3,2,1,0:T(8,128)S(1)} custom-call(bf16[2880,640]{1,0:T(8,128)(2,1)} %codes_hbm.1, f32[2880]{0:T(1024)S(1)} %copy-done, f32[640]{0:T(1024)S(1)} %copy-done.1, s32[64]{0:T(128)S(1)} %copy-done.2), custom_call_target="tpu_custom_call" | custom-call | tf_op jit(solution)/shard_map/spectra_cross/pallas_call | solution.py:379
  62.9 1.4 %copy.5 = f32[8,2,89,89]{3,1,2,0:T(2,128)} copy(f32[8,2,89,89]{3,2,1,0:T(8,128)S(1)} %bitcast.1) | data formatting | bytes 1013888 | tf_op jit(solution)/shard_map/slice | solution.py:415
Async XLA Ops:
  0.0 0.7 %copy-start = (f32[2880]{0:T(1024)S(1)}, f32[2880]{0:T(1024)}, u32[]{:S(2)}) copy-start(f32[2880]{0:T(1024)} %scales_hbm.1) | copy-start | bytes 34564
  0.7 0.7 %copy-start.1 = (f32[640]{0:T(1024)S(1)}, f32[640]{0:T(1024)}, u32[]{:S(2)}) copy-start(f32[640]{0:T(1024)} %weights_hbm.1) | copy-start | bytes 7684
  1.4 0.7 %copy-start.2 = (s32[64]{0:T(128)S(1)}, s32[64]{0:T(128)}, u32[]{:S(2)}) copy-start(s32[64]{0:T(128)} %freq_ref.1) | copy-start | bytes 772

commit v2 on v1

--- a/solution.py
+++ b/solution.py
@@ -16,6 +16,7 @@
 NT = 4
 NZ = 4
 QUARTERS = 4
+PIECES = 2
 ZSETS = ((0, 3), (1, 2))
 MESH = pl.DeviceIdType.MESH
 
@@ -30,20 +31,27 @@
     return (cosine_table, sine_table)
 
 
-def turn_cosine(turn):
-    left = 64 - jnp.minimum(turn, NFFT - turn)
-    x = left.astype(jnp.float32) * (2.0 * math.pi / NFFT)
+def turn_waves(turn):
+    angle = turn.astype(jnp.float32) * (2.0 * math.pi / NFFT)
+    quarter = (turn + NFFT // 8) // (NFFT // 4)
+    count = quarter.astype(jnp.float32)
+    x = ((angle - count * 1.5703125) - count * 4.837512969970703125e-4) - count * 7.549789948768648e-8
     y = x * x
-    poly = jnp.full_like(x, -1.0 / 39916800.0)
-    for c in (1.0 / 362880.0, -1.0 / 5040.0, 1.0 / 120.0, -1.0 / 6.0, 1.0):
-        poly = poly * y + c
-    return x * poly
+    sine = x + x * y * (-1.0 / 6.0 + y * (1.0 / 120.0 + y * (-1.0 / 5040.0 + y * (1.0 / 362880.0))))
+    cosine = 1.0 + y * (-0.5 + y * (1.0 / 24.0 + y * (-1.0 / 720.0 + y * (1.0 / 40320.0))))
+    swap = quarter % 2 == 1
+    low = jnp.where(swap, sine, cosine)
+    high = jnp.where(swap, cosine, sine)
+    return (
+        jnp.where((quarter + 1) % 4 >= 2, -low, low),
+        jnp.where(quarter % 4 >= 2, -high, high),
+    )
 
 
 def kernel(
     total_points,
-    codes_hbm, scales_hbm, weights_hbm, freq_ref, out_ref,
-    codes_ref, scales_v, weights_v, spread, vals, table, sbuf, rbuf, spbuf, sprecv, stage,
+    codes_hbm, scales_hbm, weights_hbm, freq_hbm, out_ref,
+    codes_ref, scales_v, weights_v, freq_ref, spread, vals, table, sbuf, rbuf, spbuf, sprecv, stage,
     part, corebuf, summed, zbuf, gath,
     load_s, halo_s, halo_r, tm_s, tm_r, sp_s, sp_r, core_s, core_r, z_s, z_r, g_s, g_r,
 ):
@@ -71,6 +79,7 @@
 
     load_scales = pltpu.make_async_copy(scales_hbm, scales_v, load_s.at[3])
     load_weights = pltpu.make_async_copy(weights_hbm, weights_v, load_s.at[4])
+    load_freq = pltpu.make_async_copy(freq_hbm, freq_ref, load_s.at[5])
     load_edge = load(edge_at, HALF, 0)
     load_early = load(early_at, early, 1)
     load_late = load(late_at, late, 2)
@@ -80,6 +89,7 @@
     pl.semaphore_signal(barrier, inc=1, device_id=(t, partner), device_id_type=MESH)
     for d in range(1, NZ):
         pl.semaphore_signal(barrier, inc=1, device_id=(t, (z + d) % NZ * 2 + c), device_id_type=MESH)
+    load_freq.start()
     load_scales.start()
     load_edge.start()
     load_early.start()
@@ -88,16 +98,17 @@
 
     sample = lax.broadcasted_iota(jnp.int32, (8, NFFT), 1)
     sub = lax.broadcasted_iota(jnp.int32, (8, NFFT), 0)
-    window_shape = 0.25 * (0.5 - 0.5 * turn_cosine(sample))
-    shift = (sub % 2) * (NFFT // 4)
+    window_shape = 0.25 * (0.5 - 0.5 * turn_waves(sample)[0])
 
     def octet_table(dest, q):
         bins = jnp.zeros((8, NFFT), jnp.int32)
         for j in range(4):
             dest_p = ZSETS[q % 2][j // 2] * 2 + j % 2
             bins = jnp.where(sub // 2 == j, freq_ref[dest_p * 2 * NT + dest * 2 + q // 2], bins)
-        return window_shape * turn_cosine((bins * sample + shift) % NFFT)
-
+        cosine, sine = turn_waves(bins * sample % NFFT)
+        return window_shape * jnp.where(sub % 2 == 0, cosine, -sine)
+
+    load_freq.wait()
     for dest in range(NT):
         for half in range(2):
             at = dest * 32 + half * 16
@@ -106,9 +117,9 @@
 
     load_scales.wait()
     for g in range(-(-rows // HOP)):
-        count = min(HOP, rows - g * HOP)
-        line = scales_v[g * HOP:g * HOP + count].reshape(1, count)
-        spread[g * HOP:g * HOP + count, :] = jnp.broadcast_to(line, (LANES, count)).T
+        size = min(HOP, rows - g * HOP)
+        line = scales_v[g * HOP:g * HOP + size].reshape(1, size)
+        spread[g * HOP:g * HOP + size, :] = jnp.broadcast_to(line, (LANES, size)).T
 
     offset = odd * HALF
 
@@ -242,8 +253,9 @@
 
         lax.fori_loop(at, at + count, one, 0)
 
-    def gram(q, j):
-        at = slice(j * 2 * SLOTS, (j + 1) * 2 * SLOTS)
+    def gram(q, s, side):
+        j = s * 2 + side
+        at = pl.ds(pl.multiple_of(j * 2 * SLOTS, 2 * SLOTS), 2 * SLOTS)
         stacked = jnp.concatenate(
             [stage[lane, at, :].astype(jnp.bfloat16) for lane in range(lane_tiles)], axis=1
         )
@@ -254,100 +266,121 @@
         )
         real = prod[:SLOTS, :LANES] + prod[SLOTS:, LANES:]
         imag = prod[:SLOTS, LANES:] - prod[SLOTS:, :LANES]
-        part[q, j % 2, j // 2] = real + imag
-
-    def to_core(q):
+        part[q, side, s] = real + imag
+
+    def rows_of(h):
+        return pl.ds(h * SLOTS // PIECES, SLOTS // PIECES)
+
+    def to_core(q, h):
         return pltpu.make_async_remote_copy(
-            src_ref=part.at[q, 1 - c], dst_ref=corebuf.at[q],
-            send_sem=core_s.at[q], recv_sem=core_r.at[q],
+            src_ref=part.at[q, 1 - c, :, rows_of(h)], dst_ref=corebuf.at[q, :, rows_of(h)],
+            send_sem=core_s.at[q, h], recv_sem=core_r.at[q, h],
             device_id=(t, partner), device_id_type=MESH,
         )
 
-    def to_z(q, s, source):
+    def to_z(q, s, h, source):
         return pltpu.make_async_remote_copy(
-            src_ref=summed.at[q, s], dst_ref=zbuf.at[q, source],
-            send_sem=z_s.at[q, s], recv_sem=z_r.at[q, source],
+            src_ref=summed.at[q, s, rows_of(h)], dst_ref=zbuf.at[q, source, rows_of(h)],
+            send_sem=z_s.at[q, s, h], recv_sem=z_r.at[q, source, h],
             device_id=(t, ZSETS[q % 2][s] * 2 + c), device_id_type=MESH,
         )
 
-    def to_tm(k, d, source):
+    def to_tm(k, h, d, source):
         return pltpu.make_async_remote_copy(
-            src_ref=gath.at[source, k], dst_ref=gath.at[source, k],
-            send_sem=g_s.at[k, d - 1], recv_sem=g_r.at[k, d - 1],
+            src_ref=gath.at[source, k, rows_of(h)], dst_ref=gath.at[source, k, rows_of(h)],
+            send_sem=g_s.at[k, h, d - 1], recv_sem=g_r.at[k, h, d - 1],
             device_id=(t ^ d, p), device_id_type=MESH,
         )
 
-    def receive(q):
+    def receive(q, pieces):
+        for piece in pieces:
+            for d in partners:
+                exchange(q, piece, d, t ^ d).wait_recv()
+                unpack(rbuf, q, t ^ d, piece)
+
+    def own(q):
         for piece in range(3):
             unpack(sbuf, q, t, piece)
-        for piece in range(3):
-            for d in partners:
-                exchange(q, piece, d, t ^ d).wait_recv()
-                unpack(rbuf, q, t ^ d, piece)
-        h = q // 2
+
+    def straddling(q):
         if q % 2 == 0:
             for d in partners:
                 source = t ^ d
 
                 @pl.when((source == 1) | (source == 2))
                 def _():
-                    straddle(h, d, source).wait_recv()
-        both = sprecv[h, 0].astype(jnp.float32) + sprecv[h, 1].astype(jnp.float32)
+                    straddle(q // 2, d, source).wait_recv()
+        both = sprecv[q // 2, 0].astype(jnp.float32) + sprecv[q // 2, 1].astype(jnp.float32)
         at = q % 2 * 8
         place(2 * blocks, both[at:at + 8])
 
-    def core_stage(q):
-        to_core(q).wait()
+    def core_stage(q, h):
+        to_core(q, h).wait()
         for s in range(2):
-            summed[q, s] = part[q, c, s] + corebuf[q, s]
+            at = rows_of(h)
+            summed[q, s, at] = part[q, c, s, at] + corebuf[q, s, at]
 
             @pl.when(z != ZSETS[q % 2][s])
             def _():
-                to_z(q, s, z).start()
-
-    def z_stage(q):
+                to_z(q, s, h, z).start()
+
+    def at_home(q):
+        return (z == ZSETS[q % 2][0]) | (z == ZSETS[q % 2][1])
+
+    def z_stage(q, h):
         for s in range(2):
             home = ZSETS[q % 2][s]
 
             @pl.when(z == home)
             def _():
-                total = summed[q, s]
+                at = rows_of(h)
+                total = summed[q, s, at]
                 for other in range(NZ):
                     if other != home:
-                        to_z(q, s, other).wait_recv()
-                        total = total + zbuf[q, other]
-                gath[t, q // 2] = total
-                for d in partners:
-                    to_tm(q // 2, d, t).start()
-
-    def finish(k):
-        for d in partners:
-            to_tm(k, d, t ^ d).wait_recv()
-
-        def one(s, carry):
-            ordered = gath[s, k]
-            fill = jnp.zeros((LANES - SLOTS, LANES), jnp.float32)
-            mirrored = jnp.concatenate([ordered, fill], axis=0).T[:SLOTS]
-            out_ref[s * 2 + k, 0] = 0.5 * (ordered + mirrored)
-            out_ref[s * 2 + k, 1] = 0.5 * (ordered - mirrored)
-            return carry
-
-        lax.fori_loop(0, NT, one, 0)
+                        to_z(q, s, h, other).wait_recv()
+                        total = total + zbuf[q, other, at]
+                gath[t, q // 2, at] = total
+
+    def spread_result(q, h):
+        @pl.when(at_home(q))
+        def _():
+            for d in partners:
+                to_tm(q // 2, h, d, t).start()
 
     for q in range(QUARTERS):
+        last = q == QUARTERS - 1
         if 0 < q < QUARTERS - 1:
             for piece in range(3):
                 send(q + 1, piece)
-        receive(q)
-        for j in (0, 2, 1, 3):
-            gram(q, j)
-        to_core(q).start()
+        own(q)
+        receive(q, (0,))
+        straddling(q)
         if q >= 1:
-            z_stage(q - 1)
-        core_stage(q)
-    z_stage(QUARTERS - 1)
-    finish(0)
-    finish(1)
+            for h in range(PIECES):
+                z_stage(q - 1, h)
+        receive(q, (1, 2))
+        if last:
+            for early_q in range(QUARTERS - 1):
+                for h in range(PIECES):
+                    spread_result(early_q, h)
+        for s in range(2):
+            gram(q, s, 1 - c)
+        for h in range(PIECES):
+            to_core(q, h).start()
+        for s in range(2):
+            gram(q, s, c)
+        for h in range(PIECES):
+            core_stage(q, h)
+    for h in range(PIECES):
+        z_stage(QUARTERS - 1, h)
+        spread_result(QUARTERS - 1, h)
+
+    for k in range(2):
+        for h in range(PIECES):
+            for d in partners:
+                to_tm(k, h, d, t ^ d).wait_recv()
+        for s in range(NT):
+            out_ref[s * 2 + k] = gath[s, k]
 
     halo_copy(halo_to).wait_send()
     for q in range(QUARTERS):
@@ -357,34 +390,61 @@
         for s in range(2):
             @pl.when(z != ZSETS[q % 2][s])
             def _():
-                to_z(q, s, z).wait_send()
+                for h in range(PIECES):
+                    to_z(q, s, h, z).wait_send()
     for k in range(2):
-        for d in partners:
-            to_tm(k, d, t).wait_send()
+        for h in range(PIECES):
+            for d in partners:
+                to_tm(k, h, d, t).wait_send()
 
     @pl.when(middle)
     def _():
         for h in range(2):
             for d in partners:
                 straddle(h, d, t).wait_send()
+
+
+def finish(sums_ref, out_hbm, both, sems):
+    freqs = sums_ref.shape[0]
+    count = out_hbm.shape[1]
+
+    def copy(part):
+        size = freqs // 2 * 2 * count
+        at = pl.ds(part * size, size)
+        return pltpu.make_async_copy(both.at[at], out_hbm.at[at], sems.at[part])
+
+    for part in range(2):
+        for f in range(part * freqs // 2, (part + 1) * freqs // 2):
+            ordered = sums_ref[f]
+            fill = jnp.zeros((LANES - SLOTS, LANES), jnp.float32)
+            mirrored = jnp.concatenate([ordered, fill], axis=0).T[:SLOTS]
+            first = f * 2 * count
+            both[pl.ds(first, count, stride=2), :] = 0.5 * (ordered + mirrored)[:count, :count]
+            both[pl.ds(first + 1, count, stride=2), :] = 0.5 * (ordered - mirrored)[:count, :count]
+        copy(part).start()
+    for part in range(2):
+        copy(part).wait()
 
 
 def fused(codes, scales, weights, freq_indices, total_points):
     rows, points = codes.shape
     blocks = rows // HOP
     pairs = blocks // 2
+    count = rows * NT // HOP - 1
     f32, bf16 = jnp.float32, jnp.bfloat16
     dma = pltpu.SemaphoreType.DMA
-    hbm = pl.BlockSpec(memory_space=pl.ANY)
-    full = pl.pallas_call(
+    hbm = pl.BlockSpec(memory_space=pltpu.HBM)
+    vmem = pl.BlockSpec(memory_space=pltpu.VMEM)
+    sums = pl.pallas_call(
         functools.partial(kernel, total_points),
-        out_shape=jax.ShapeDtypeStruct((2 * NT, 2, SLOTS, LANES), f32),
-        in_specs=[hbm, hbm, hbm, pl.BlockSpec(memory_space=pltpu.SMEM)],
-        out_specs=pl.BlockSpec(memory_space=pltpu.VMEM),
+        out_shape=jax.ShapeDtypeStruct((2 * NT, SLOTS, LANES), f32),
+        in_specs=[hbm, hbm, hbm, hbm],
+        out_specs=vmem,
         scratch_shapes=[
             pltpu.VMEM((rows, points), bf16),
             pltpu.VMEM((rows,), f32),
             pltpu.VMEM((points,), f32),
+            pltpu.SMEM(freq_indices.shape, jnp.int32),
             pltpu.VMEM((rows, LANES), f32),
             pltpu.VMEM((rows + HALF, points), bf16),
             pltpu.VMEM((2 * NT * QUARTERS * 4, NFFT), bf16),
@@ -398,21 +458,28 @@
             pltpu.VMEM((QUARTERS, 2, SLOTS, LANES), f32),
             pltpu.VMEM((QUARTERS, NZ, SLOTS, LANES), f32),
             pltpu.VMEM((NT, 2, SLOTS, LANES), f32),
-            dma((5,)),
+            dma((6,)),
             dma, dma,
             dma((QUARTERS, 3, NT - 1)), dma((QUARTERS, 3, NT - 1)),
             dma((2, NT - 1)), dma((2, NT - 1)),
-            dma((QUARTERS,)), dma((QUARTERS,)),
-            dma((QUARTERS, 2)), dma((QUARTERS, NZ)),
-            dma((2, NT - 1)), dma((2, NT - 1)),
+            dma((QUARTERS, PIECES)), dma((QUARTERS, PIECES)),
+            dma((QUARTERS, 2, PIECES)), dma((QUARTERS, NZ, PIECES)),
+            dma((2, PIECES, NT - 1)), dma((2, PIECES, NT - 1)),
         ],
         compiler_params=pltpu.CompilerParams(
-            collective_id=0, has_side_effects=True, vmem_limit_bytes=52 * 2**20
+            collective_id=0, has_side_effects=True, vmem_limit_bytes=56 * 2**20
         ),
         name="spectra_cross",
     )(codes, scales, weights, freq_indices)
-    count = rows * NT // HOP - 1
-    return full[:, :, :count, :count]
+    full = pl.pallas_call(
+        finish,
+        out_shape=jax.ShapeDtypeStruct((2 * NT * 2 * count, count), f32),
+        in_specs=[vmem],
+        out_specs=hbm,
+        scratch_shapes=[pltpu.VMEM((2 * NT * 2 * count, count), f32), dma((2,))],
+        name="hermitian_parts",
+    )(sums)
+    return full.reshape(2 * NT, count, 2, count).transpose(0, 2, 1, 3)
 
 
 def cross_matrices(stacked):

time: 65.3 us -> 61.2 us (0.937); the launches traced: 64.3 us -> 61 us
  local copies, waits for them, and re-layouts: 3.47 us -> 0 us
    unnamed x6 -> x0, local copies, waits for them, and re-layouts: 2.05 us -> none
    pallas_call x0 -> x1, Pallas kernels: none -> 1.99 us  [fused(): pl.pallas_call(finish, out_shape=jax.ShapeDtypeStruct((2 * NT * 2 * count...]
    pallas_call x1, Pallas kernels: 60.8 us -> 59 us  [fused(): pl.pallas_call(functools.partial(kernel, total_points), out_shape=jax.Sha...]
    slice x1 -> x0, local copies, waits for them, and re-layouts: 1.43 us -> none  [fused(): return full[:, :, :count, :count]]
where the time goes in v2:
time: 61.2 us; the launch traced here: 61 us
  Pallas kernels  61 us (100%)
    pallas_call x1, Pallas kernels, fused(): pl.pallas_call(functools.partial(kernel, total_points), out_shape=jax.Sha...  59 us
    pallas_call x1, Pallas kernels, fused(): pl.pallas_call(finish, out_shape=jax.ShapeDtypeStruct((2 * NT * 2 * count...  1.99 us

profile of v2, /device:TPU:8, one launch (start us, length us, event | category | flops | bytes accessed | tf_op | source)
XLA Modules:
  0.0 61.0 jit_solution(9441867293488669101)
XLA Ops:
  0.0 59.0 %spectra_cross.1.sums_ref = f32[8,96,128]{2,1,0:T(8,128)} custom-call(bf16[2880,640]{1,0:T(8,128)(2,1)} %codes_hbm.1, f32[2880]{0:T(1024)} %scales_hbm.1, f32[640]{0:T(1024)} %weights_hbm.1, s32[64]{0:T(128)} %freq_hbm.1), custom_call_target="tpu_custom_call" | custom-call | tf_op jit(solution)/shard_map/spectra_cross/pallas_call | solution.py:438
  59.0 2.0 %hermitian_parts.1 = f32[1424,89]{1,0:T(8,128)} custom-call(f32[8,96,128]{2,1,0:T(8,128)} %spectra_cross.1.sums_ref), custom_call_target="tpu_custom_call" | custom-call | tf_op jit(solution)/shard_map/hermitian_parts/pallas_call | solution.py:474

commit v3 on v2

--- a/solution.py
+++ b/solution.py
@@ -51,9 +51,9 @@
 def kernel(
     total_points,
     codes_hbm, scales_hbm, weights_hbm, freq_hbm, out_ref,
-    codes_ref, scales_v, weights_v, freq_ref, spread, vals, table, sbuf, rbuf, spbuf, sprecv, stage,
+    codes_ref, scales_v, weights_v, freq_ref, spread, vals, table, sbuf, rbuf, hops, spbuf, sprecv, stage,
     part, corebuf, summed, zbuf, gath,
-    load_s, halo_s, halo_r, tm_s, tm_r, sp_s, sp_r, core_s, core_r, z_s, z_r, g_s, g_r,
+    load_s, halo_s, halo_r, tm_s, tm_r, hop_s, hop_r, sp_s, sp_r, core_s, core_r, z_s, z_r, g_s, g_r,
 ):
     rows, points = codes_ref.shape
     t = lax.axis_index("tm")
@@ -186,25 +186,42 @@
             device_id=(t ^ d, p), device_id_type=MESH,
         )
 
-    def straddle(h, d, source):
-        return pltpu.make_async_remote_copy(
-            src_ref=spbuf.at[h, t ^ d],
-            dst_ref=sprecv.at[h, source - 1],
-            send_sem=sp_s.at[h, d - 1], recv_sem=sp_r.at[h, d - 1],
+    middle = (t == 1) | (t == 2)
+    outer = (t == 0) | (t == 3)
+
+    def owner(lane):
+        if 2 * lane + 1 == lane_tiles:
+            return (NT - 1) * (1 - c)
+        return (NT - 1) * int(2 * lane + 1 > lane_tiles)
+
+    def lanes(lane):
+        return pl.ds(lane * LANES, LANES)
+
+    def hop_copy(lane, source, dest):
+        return pltpu.make_async_remote_copy(
+            src_ref=vals.at[pl.ds(pl.multiple_of(odd * (padded - HOP), HOP), HOP), lanes(lane)],
+            dst_ref=hops.at[pl.ds(pl.multiple_of((source - 1) * HOP, HOP), HOP), lanes(lane)],
+            send_sem=hop_s.at[lane], recv_sem=hop_r.at[source - 1, lane],
+            device_id=(dest, p), device_id_type=MESH,
+        )
+
+    def straddle(lane, d):
+        return pltpu.make_async_remote_copy(
+            src_ref=spbuf.at[t ^ d, :, :, lanes(lane)],
+            dst_ref=sprecv.at[:, :, lanes(lane)],
+            send_sem=sp_s.at[lane, d - 1], recv_sem=sp_r.at[lane],
             device_id=(t ^ d, p), device_id_type=MESH,
         )
-
-    middle = (t == 1) | (t == 2)
-
-    def send_straddle(h):
-        @pl.when(middle)
-        def _():
-            for d in partners:
-                straddle(h, d, t).start()
 
     def send(q, piece):
         for d in partners:
             exchange(q, piece, d, t).start()
+
+
+    @pl.when(middle)
+    def _():
+        for lane in range(lane_tiles):
+            hop_copy(lane, t, owner(lane)).start()
 
     lax.fori_loop(cuts[0], cuts[1], spectra, 0)
     send(0, 0)
@@ -216,20 +233,25 @@
     lax.fori_loop(cuts[2], cuts[3], spectra, 0)
     send(0, 2)
 
-    @pl.when(middle)
+    @pl.when(outer)
     def _():
-        hop = pl.ds(pl.multiple_of(odd * (padded - HOP), HOP), HOP)
-        side = jnp.where(odd == 1, table[:, :HOP].astype(jnp.float32), table[:, HOP:].astype(jnp.float32))
-        result = jnp.dot(side.astype(jnp.bfloat16), vals[hop, :], preferred_element_type=jnp.float32)
+        for lane in range(lane_tiles):
+            @pl.when(t == owner(lane))
+            def _():
+                for source in (1, 2):
+                    hop_copy(lane, source, owner(lane)).wait_recv()
+        result = jnp.dot(table[...], hops[...], preferred_element_type=jnp.float32)
         result = (result * root_weight).astype(jnp.bfloat16)
         for dest in range(NT):
             for h in range(2):
-                spbuf[h, dest] = result[dest * 32 + h * 16:dest * 32 + h * 16 + 16]
-        for h in range(2):
-            sprecv[h, t - 1] = spbuf[h, t]
-
-    for h in range(2):
-        send_straddle(h)
+                spbuf[dest, h] = result[dest * 32 + h * 16:dest * 32 + h * 16 + 16]
+        for lane in range(lane_tiles):
+            @pl.when(t == owner(lane))
+            def _():
+                for d in partners:
+                    straddle(lane, d).start()
+                sprecv[:, :, lanes(lane)] = spbuf[t, :, :, lanes(lane)]
+
     for piece in range(3):
         send(1, piece)
 
@@ -303,16 +325,13 @@
             unpack(sbuf, q, t, piece)
 
     def straddling(q):
-        if q % 2 == 0:
-            for d in partners:
-                source = t ^ d
-
-                @pl.when((source == 1) | (source == 2))
+        if q == 0:
+            for lane in range(lane_tiles):
+                @pl.when(t != owner(lane))
                 def _():
-                    straddle(q // 2, d, source).wait_recv()
-        both = sprecv[q // 2, 0].astype(jnp.float32) + sprecv[q // 2, 1].astype(jnp.float32)
+                    straddle(lane, 1).wait_recv()
         at = q % 2 * 8
-        place(2 * blocks, both[at:at + 8])
+        place(2 * blocks, sprecv[q // 2].astype(jnp.float32)[at:at + 8])
 
     def core_stage(q, h):
         to_core(q, h).wait()
@@ -397,11 +416,15 @@
             for d in partners:
                 to_tm(k, h, d, t).wait_send()
 
-    @pl.when(middle)
-    def _():
-        for h in range(2):
+    for lane in range(lane_tiles):
+        @pl.when(middle)
+        def _():
+            hop_copy(lane, t, owner(lane)).wait_send()
+
+        @pl.when(t == owner(lane))
+        def _():
             for d in partners:
-                straddle(h, d, t).wait_send()
+                straddle(lane, d).wait_send()
 
 
 def finish(sums_ref, out_hbm, both, sems):
@@ -430,11 +453,15 @@
     rows, points = codes.shape
     blocks = rows // HOP
     pairs = blocks // 2
+    lane_tiles = points // LANES
     count = rows * NT // HOP - 1
     f32, bf16 = jnp.float32, jnp.bfloat16
     dma = pltpu.SemaphoreType.DMA
     hbm = pl.BlockSpec(memory_space=pltpu.HBM)
     vmem = pl.BlockSpec(memory_space=pltpu.VMEM)
+    pinned = [
+        pltpu.with_memory_space_constraint(x, pltpu.HBM) for x in (codes, scales, weights, freq_indices)
+    ]
     sums = pl.pallas_call(
         functools.partial(kernel, total_points),
         out_shape=jax.ShapeDtypeStruct((2 * NT, SLOTS, LANES), f32),
@@ -450,8 +477,9 @@
             pltpu.VMEM((2 * NT * QUARTERS * 4, NFFT), bf16),
             pltpu.VMEM((QUARTERS, NT, pairs, 16, points), bf16),
             pltpu.VMEM((QUARTERS, NT, pairs, 16, points), bf16),
-            pltpu.VMEM((2, NT, 16, points), bf16),
-            pltpu.VMEM((2, 2, 16, points), bf16),
+            pltpu.VMEM((NFFT, points), bf16),
+            pltpu.VMEM((NT, 2, 16, points), bf16),
+            pltpu.VMEM((2, 16, points), bf16),
             pltpu.VMEM((points // LANES, 8 * SLOTS, LANES), f32),
             pltpu.VMEM((QUARTERS, 2, 2, SLOTS, LANES), f32),
             pltpu.VMEM((QUARTERS, 2, SLOTS, LANES), f32),
@@ -461,16 +489,17 @@
             dma((6,)),
             dma, dma,
             dma((QUARTERS, 3, NT - 1)), dma((QUARTERS, 3, NT - 1)),
-            dma((2, NT - 1)), dma((2, NT - 1)),
+            dma((lane_tiles,)), dma((2, lane_tiles)),
+            dma((lane_tiles, NT - 1)), dma((lane_tiles,)),
             dma((QUARTERS, PIECES)), dma((QUARTERS, PIECES)),
             dma((QUARTERS, 2, PIECES)), dma((QUARTERS, NZ, PIECES)),
             dma((2, PIECES, NT - 1)), dma((2, PIECES, NT - 1)),
         ],
         compiler_params=pltpu.CompilerParams(
-            collective_id=0, has_side_effects=True, vmem_limit_bytes=56 * 2**20
+            collective_id=0, has_side_effects=True, vmem_limit_bytes=40 * 2**20
         ),
         name="spectra_cross",
-    )(codes, scales, weights, freq_indices)
+    )(*pinned)
     full = pl.pallas_call(
         finish,
         out_shape=jax.ShapeDtypeStruct((2 * NT * 2 * count, count), f32),
@@ -478,7 +507,7 @@
         out_specs=hbm,
         scratch_shapes=[pltpu.VMEM((2 * NT * 2 * count, count), f32), dma((2,))],
         name="hermitian_parts",
-    )(sums)
+    )(pltpu.with_memory_space_constraint(sums, pltpu.VMEM))
     return full.reshape(2 * NT, count, 2, count).transpose(0, 2, 1, 3)
 
 

time: 61.2 us -> 59.6 us (0.974)
  Pallas kernels: 61 us -> 59.5 us
    pallas_call x1, Pallas kernels: 1.99 us -> 1 us  [fused(): pl.pallas_call(finish, out_shape=jax.ShapeDtypeStruct((2 * NT * 2 * count...]
where the time goes in v3:
time: 59.6 us; the launch traced here: 59.5 us
  Pallas kernels  59.5 us (100%)
    pallas_call x1, Pallas kernels, fused(): pl.pallas_call(functools.partial(kernel, total_points), out_shape=jax.Sha...  58.5 us

profile of v3, /device:TPU:8, one launch (start us, length us, event | category | flops | bytes accessed | tf_op | source)
XLA Modules:
  0.0 59.5 jit_solution(363626556118200173)
XLA Ops:
  0.0 58.5 %spectra_cross.1.sums_ref = f32[8,96,128]{2,1,0:T(8,128)S(1)} custom-call(bf16[2880,640]{1,0:T(8,128)(2,1)} %codes_hbm.1, f32[2880]{0:T(1024)} %scales_hbm.1, f32[640]{0:T(1024)} %weights_hbm.1, s32[64]{0:T(128)} %freq_hbm.1), custom_call_target="tpu_custom_call" | custom-call | tf_op jit(solution)/shard_map/spectra_cross/pallas_call | solution.py:465
  58.5 1.0 %hermitian_parts.1 = f32[1424,89]{1,0:T(8,128)} custom-call(f32[8,96,128]{2,1,0:T(8,128)S(1)} %spectra_cross.1.sums_ref), custom_call_target="tpu_custom_call" | custom-call | tf_op jit(solution)/shard_map/hermitian_parts/pallas_call | solution.py:503

commit v4 on v3

--- a/solution.py
+++ b/solution.py
@@ -13,11 +13,20 @@
 HALF = HOP // 2
 LANES = 128
 SLOTS = 96
+KEPT = 72
 NT = 4
 NZ = 4
 QUARTERS = 4
-PIECES = 2
+FULL = 3
+ROW_PARTS = ((0, 72),)
+PIECES = len(ROW_PARTS)
 ZSETS = ((0, 3), (1, 2))
+ORDERS = (
+    ((0, 0), (0, 1), (3, 0), (3, 1)),
+    ((1, 0), (1, 1), (2, 0), (2, 1)),
+    ((0, 0), (0, 1), (3, 0), (3, 1)),
+    ((1, 1), (2, 0), (1, 0), (2, 1)),
+)
 MESH = pl.DeviceIdType.MESH
 
 
@@ -48,12 +57,37 @@
     )
 
 
+def fold(matrix):
+    lane = lax.broadcasted_iota(jnp.int32, (KEPT, LANES), 1)
+    rest = jnp.zeros((LANES - (SLOTS - KEPT), LANES), jnp.float32)
+    turned = jnp.concatenate([matrix[KEPT:], rest], axis=0).T
+    corner = turned[KEPT:SLOTS]
+    corners = jnp.concatenate([pltpu.roll(corner, LANES - 8 * m, 1) for m in (1, 2, 3)], axis=0)
+    side = pltpu.roll(turned[:KEPT], SLOTS, 1)
+    return jnp.where(lane < SLOTS, matrix[:KEPT], jnp.where(lane < LANES - 8, side, corners))
+
+
+def unfold(folded):
+    lane = lax.broadcasted_iota(jnp.int32, (KEPT, LANES), 1)
+    top = jnp.where(lane < SLOTS, folded, 0.0)
+    side = jnp.where(lane < SLOTS - KEPT, pltpu.roll(folded, LANES - SLOTS, 1), 0.0)
+    size = SLOTS - KEPT
+    corner = jnp.zeros((size, LANES), jnp.float32)
+    for m in (1, 2, 3):
+        moved = pltpu.roll(folded[(m - 1) * size:m * size], 8 * m, 1)
+        here = lane[:size]
+        corner = jnp.where((here >= 8 * m - 8) & (here < 8 * m), moved, corner)
+    rest = jnp.zeros((LANES - SLOTS, LANES), jnp.float32)
+    turned = jnp.concatenate([side, corner, rest], axis=0).T
+    return jnp.concatenate([top, turned[:size]], axis=0)
+
+
 def kernel(
     total_points,
     codes_hbm, scales_hbm, weights_hbm, freq_hbm, out_ref,
-    codes_ref, scales_v, weights_v, freq_ref, spread, vals, table, sbuf, rbuf, hops, spbuf, sprecv, stage,
-    part, corebuf, summed, zbuf, gath,
-    load_s, halo_s, halo_r, tm_s, tm_r, hop_s, hop_r, sp_s, sp_r, core_s, core_r, z_s, z_r, g_s, g_r,
+    codes_ref, scales_v, weights_v, freq_ref, spread, vals, table, sbuf, rbuf, sfirst, rfirst, slast, rlast, hops, spbuf, sprecv, stage,
+    part, corebuf, summed, zbuf, part2, corebuf2, summed2, zbuf2, homebuf, gath,
+    load_s, halo_s, halo_r, tm_s, tm_r, first_s, first_r, last_s, last_r, hop_s, hop_r, sp_s, sp_r, core_s, core_r, z_s, z_r, core2_s, core2_r, z2_s, z2_r, home_s, home_r, g_s, g_r,
 ):
     rows, points = codes_ref.shape
     t = lax.axis_index("tm")
@@ -103,7 +137,7 @@
     def octet_table(dest, q):
         bins = jnp.zeros((8, NFFT), jnp.int32)
         for j in range(4):
-            dest_p = ZSETS[q % 2][j // 2] * 2 + j % 2
+            dest_p = ORDERS[q][j][0] * 2 + ORDERS[q][j][1]
             bins = jnp.where(sub // 2 == j, freq_ref[dest_p * 2 * NT + dest * 2 + q // 2], bins)
         cosine, sine = turn_waves(bins * sample % NFFT)
         return window_shape * jnp.where(sub % 2 == 0, cosine, -sine)
@@ -158,18 +192,39 @@
         window = vals[pl.ds(pl.multiple_of(i * HOP, HOP), NFFT), :]
         return jnp.dot(table[...], window, preferred_element_type=jnp.float32) * root_weight
 
-    def spectra(j, carry):
-        jj = odd * (pairs - 1 - j) + (1 - odd) * j
-        first = spectrum(2 * jj)
-        second = spectrum(2 * jj + 1)
+    def octets(result, dest, q):
+        return result[dest * 32 + q * 8:dest * 32 + q * 8 + 8]
+
+    def pair_tiles(jj, first, second):
         for dest in range(NT):
-            for q in range(QUARTERS):
-                at = slice(dest * 32 + q * 8, dest * 32 + q * 8 + 8)
-                both = jnp.concatenate([first[at], second[at]], axis=0)
+            for q in range(FULL):
+                both = jnp.concatenate([octets(first, dest, q), octets(second, dest, q)], axis=0)
                 sbuf[q, dest, jj] = both.astype(jnp.bfloat16)
+
+    def spectra(u, carry):
+        low = odd * (pairs - 2 - 2 * u) + (1 - odd) * 2 * u
+        results = [spectrum(2 * low + r) for r in range(4)]
+        pair_tiles(low, results[0], results[1])
+        pair_tiles(low + 1, results[2], results[3])
+        v = odd * (quads - 1 - u) + (1 - odd) * u
+        for dest in range(NT):
+            last = [octets(r, dest, FULL) for r in results]
+            sfirst[dest, v] = jnp.concatenate([o[:4] for o in last], axis=0).astype(jnp.bfloat16)
+            slast[dest, v] = jnp.concatenate([o[4:] for o in last], axis=0).astype(jnp.bfloat16)
         return carry
 
-    cuts = (0, 4, pairs - 1, pairs)
+    def spectra_pair():
+        jj = (1 - odd) * (pairs - 1)
+        first, second = spectrum(2 * jj), spectrum(2 * jj + 1)
+        pair_tiles(jj, first, second)
+        for dest in range(NT):
+            one, two = octets(first, dest, FULL), octets(second, dest, FULL)
+            mixed = jnp.concatenate([one[:4], two[:4], one[4:], two[4:]], axis=0)
+            sfirst[dest, quads] = mixed.astype(jnp.bfloat16)
+
+    quads = pairs // 2
+    q_cut = 2
+    cuts = (0, 2 * q_cut, pairs - 1, pairs)
     partners = (3, 1, 2)
 
     def tiles_of(who, piece):
@@ -186,6 +241,23 @@
             device_id=(t ^ d, p), device_id_type=MESH,
         )
 
+    def exchange_first(d, source):
+        return pltpu.make_async_remote_copy(
+            src_ref=sfirst.at[t ^ d], dst_ref=rfirst.at[source],
+            send_sem=first_s.at[d - 1], recv_sem=first_r.at[d - 1],
+            device_id=(t ^ d, p), device_id_type=MESH,
+        )
+
+    last_cuts = (0, 3, quads)
+
+    def exchange_last(piece, d, source):
+        at = pl.ds(last_cuts[piece], last_cuts[piece + 1] - last_cuts[piece])
+        return pltpu.make_async_remote_copy(
+            src_ref=slast.at[t ^ d, at], dst_ref=rlast.at[source, at],
+            send_sem=last_s.at[piece, d - 1], recv_sem=last_r.at[piece, d - 1],
+            device_id=(t ^ d, p), device_id_type=MESH,
+        )
+
     middle = (t == 1) | (t == 2)
     outer = (t == 0) | (t == 3)
 
@@ -223,14 +295,14 @@
         for lane in range(lane_tiles):
             hop_copy(lane, t, owner(lane)).start()
 
-    lax.fori_loop(cuts[0], cuts[1], spectra, 0)
+    lax.fori_loop(0, q_cut, spectra, 0)
     send(0, 0)
     load_late.wait()
     lax.fori_loop(late_at // HALF, (late_at + late) // HALF, dequantize, 0)
-    lax.fori_loop(cuts[1], cuts[2], spectra, 0)
+    lax.fori_loop(q_cut, quads, spectra, 0)
     send(0, 1)
     halo_copy(halo_mine).wait_recv()
-    lax.fori_loop(cuts[2], cuts[3], spectra, 0)
+    spectra_pair()
     send(0, 2)
 
     @pl.when(outer)
@@ -275,8 +347,29 @@
 
         lax.fori_loop(at, at + count, one, 0)
 
-    def gram(q, s, side):
-        j = s * 2 + side
+    def place_four(half, b, octet):
+        for lane in range(lane_tiles):
+            at = pl.ds(half * 4 * SLOTS + b, 4, stride=SLOTS)
+            stage[lane, at, :] = octet[:, lane * LANES:(lane + 1) * LANES]
+
+    def unpack_fours(source_ref, half, who, first, last):
+        base = who * blocks + who // 2 + 2 * (who % 2)
+
+        def one(v, carry):
+            tile = source_ref[who, v].astype(jnp.float32)
+            for r in range(4):
+                place_four(half, base + 4 * v + r, tile[4 * r:4 * r + 4])
+            return carry
+
+        lax.fori_loop(first, last, one, 0)
+
+    def unpack_mixed(source_ref, who):
+        base = who * blocks + who // 2 + (1 - who % 2) * 2 * (pairs - 1)
+        tile = source_ref[who, quads].astype(jnp.float32)
+        for r in range(4):
+            place_four(r // 2, base + r % 2, tile[4 * r:4 * r + 4])
+
+    def gram(j):
         at = pl.ds(pl.multiple_of(j * 2 * SLOTS, 2 * SLOTS), 2 * SLOTS)
         stacked = jnp.concatenate(
             [stage[lane, at, :].astype(jnp.bfloat16) for lane in range(lane_tiles)], axis=1
@@ -288,10 +381,10 @@
         )
         real = prod[:SLOTS, :LANES] + prod[SLOTS:, LANES:]
         imag = prod[:SLOTS, LANES:] - prod[SLOTS:, :LANES]
-        part[q, side, s] = real + imag
+        return fold(real + imag)
 
     def rows_of(h):
-        return pl.ds(h * SLOTS // PIECES, SLOTS // PIECES)
+        return pl.ds(*ROW_PARTS[h])
 
     def to_core(q, h):
         return pltpu.make_async_remote_copy(
@@ -306,6 +399,68 @@
             send_sem=z_s.at[q, s, h], recv_sem=z_r.at[q, source, h],
             device_id=(t, ZSETS[q % 2][s] * 2 + c), device_id_type=MESH,
         )
+
+    def home_of(e):
+        return (1 - e) * (2 - c) + e * (1 + c)
+
+    def to_core2(e, h):
+        return pltpu.make_async_remote_copy(
+            src_ref=part2.at[e, 1 - c, rows_of(h)], dst_ref=corebuf2.at[e, rows_of(h)],
+            send_sem=core2_s.at[e, h], recv_sem=core2_r.at[e, h],
+            device_id=(t, partner), device_id_type=MESH,
+        )
+
+    def to_z2(h, source):
+        return pltpu.make_async_remote_copy(
+            src_ref=summed2.at[0, rows_of(h)], dst_ref=zbuf2.at[source, rows_of(h)],
+            send_sem=z2_s.at[h], recv_sem=z2_r.at[source, h],
+            device_id=(t, home_of(0) * 2 + c), device_id_type=MESH,
+        )
+
+    def to_home(d, source_z, source_t):
+        return pltpu.make_async_remote_copy(
+            src_ref=summed2.at[1], dst_ref=homebuf.at[source_z, source_t],
+            send_sem=home_s.at[d], recv_sem=home_r.at[source_z, source_t],
+            device_id=(t ^ d, home_of(1) * 2 + c), device_id_type=MESH,
+        )
+
+    def gram2(e, side):
+        part2[e, side] = gram((1 - e) * (1 - side) + e * (2 + side))
+
+    def core_sum2(e, h):
+        to_core2(e, h).wait_recv()
+        at = rows_of(h)
+        summed2[e, at] = part2[e, c, at] + corebuf2[e, at]
+
+    def core_stage2(h):
+        core_sum2(0, h)
+
+        @pl.when(z != home_of(0))
+        def _():
+            to_z2(h, z).start()
+
+    def home_stage():
+        for h in range(PIECES):
+            core_sum2(1, h)
+        for d in partners:
+            to_home(d, z, t).start()
+
+        @pl.when(z != home_of(1))
+        def _():
+            to_home(0, z, t).start()
+
+    def z_stage2(h):
+        @pl.when(z == home_of(0))
+        def _():
+            at = rows_of(h)
+            total = summed2[0, at]
+            for d in range(1, NZ):
+                other = (z + d) % NZ
+                to_z2(h, other).wait_recv()
+                total = total + zbuf2[other, at]
+            gath[t, 1, at] = total
+            for d in partners:
+                to_tm(1, h, d, t).start()
 
     def to_tm(k, h, d, source):
         return pltpu.make_async_remote_copy(
@@ -334,7 +489,7 @@
         place(2 * blocks, sprecv[q // 2].astype(jnp.float32)[at:at + 8])
 
     def core_stage(q, h):
-        to_core(q, h).wait()
+        to_core(q, h).wait_recv()
         for s in range(2):
             at = rows_of(h)
             summed[q, s, at] = part[q, c, s, at] + corebuf[q, s, at]
@@ -366,11 +521,21 @@
             for d in partners:
                 to_tm(q // 2, h, d, t).start()
 
-    for q in range(QUARTERS):
-        last = q == QUARTERS - 1
-        if 0 < q < QUARTERS - 1:
+    def send_first():
+        for d in partners:
+            exchange_first(d, t).start()
+
+    def send_last():
+        for piece in range(2):
+            for d in partners:
+                exchange_last(piece, d, t).start()
+
+    for q in range(FULL):
+        if q == 1:
             for piece in range(3):
-                send(q + 1, piece)
+                send(2, piece)
+        if q == 2:
+            send_first()
         own(q)
         receive(q, (0,))
         straddling(q)
@@ -378,44 +543,63 @@
             for h in range(PIECES):
                 z_stage(q - 1, h)
         receive(q, (1, 2))
-        if last:
-            for early_q in range(QUARTERS - 1):
-                for h in range(PIECES):
-                    spread_result(early_q, h)
         for s in range(2):
-            gram(q, s, 1 - c)
+            part[q, 1 - c, s] = gram(2 * s + 1 - c)
         for h in range(PIECES):
             to_core(q, h).start()
         for s in range(2):
-            gram(q, s, c)
+            part[q, c, s] = gram(2 * s + c)
         for h in range(PIECES):
             core_stage(q, h)
+
+    send_last()
+    unpack_fours(sfirst, 0, t, 0, quads)
+    unpack_mixed(sfirst, t)
+    unpack_fours(slast, 1, t, 0, quads)
+    straddling(FULL)
+    for d in partners:
+        exchange_first(d, t ^ d).wait_recv()
+        unpack_fours(rfirst, 0, t ^ d, 0, quads)
+        unpack_mixed(rfirst, t ^ d)
+    gram2(0, 1 - c)
     for h in range(PIECES):
-        z_stage(QUARTERS - 1, h)
-        spread_result(QUARTERS - 1, h)
-
-    for k in range(2):
-        for h in range(PIECES):
-            for d in partners:
-                to_tm(k, h, d, t ^ d).wait_recv()
-        for s in range(NT):
-            out_ref[s * 2 + k] = gath[s, k]
-
+        to_core2(0, h).start()
+    gram2(0, c)
+    for piece in range(2):
+        for d in partners:
+            exchange_last(piece, d, t ^ d).wait_recv()
+            unpack_fours(rlast, 1, t ^ d, last_cuts[piece], last_cuts[piece + 1])
+        if piece == 0:
+            for h in range(PIECES):
+                core_stage2(h)
+                spread_result(0, h)
+                spread_result(1, h)
+    gram2(1, 1 - c)
+    for h in range(PIECES):
+        to_core2(1, h).start()
+    gram2(1, c)
+    home_stage()
+    for h in range(PIECES):
+        z_stage(2, h)
+        spread_result(2, h)
+    for h in range(PIECES):
+        z_stage2(h)
     halo_copy(halo_to).wait_send()
-    for q in range(QUARTERS):
+    for d in partners:
+        exchange_first(d, t).wait_send()
+        for piece in range(2):
+            exchange_last(piece, d, t).wait_send()
+    for q in range(FULL):
         for piece in range(3):
             for d in partners:
                 exchange(q, piece, d, t).wait_send()
+        for h in range(PIECES):
+            to_core(q, h).wait_send()
         for s in range(2):
             @pl.when(z != ZSETS[q % 2][s])
             def _():
                 for h in range(PIECES):
                     to_z(q, s, h, z).wait_send()
-    for k in range(2):
-        for h in range(PIECES):
-            for d in partners:
-                to_tm(k, h, d, t).wait_send()
-
     for lane in range(lane_tiles):
         @pl.when(middle)
         def _():
@@ -425,6 +609,56 @@
         def _():
             for d in partners:
                 straddle(lane, d).wait_send()
+
+    for h in range(PIECES):
+        to_core2(0, h).wait_send()
+
+        @pl.when(z != home_of(0))
+        def _():
+            to_z2(h, z).wait_send()
+
+        for d in partners:
+            to_tm(0, h, d, t).wait_send()
+
+    def gathered(k):
+        out_ref[t * 2 + k] = unfold(gath[t, k])
+        for d in (1, 2, 3):
+            for h in range(PIECES):
+                to_tm(k, h, d, t ^ d).wait_recv()
+            out_ref[(t ^ d) * 2 + k] = unfold(gath[t ^ d, k])
+
+    gathered(0)
+
+    @pl.when(z != home_of(1))
+    def _():
+        gathered(1)
+        for h in range(PIECES):
+            for d in partners:
+                to_tm(1, h, d, t).wait_send()
+
+    @pl.when(z == home_of(1))
+    def _():
+        for d in range(NT):
+            source = t ^ d
+            if d == 0:
+                total = summed2[1]
+            else:
+                to_home(d, z, source).wait_recv()
+                total = homebuf[z, source]
+            for step in range(1, NZ):
+                other = (z + step) % NZ
+                to_home(d, other, source).wait_recv()
+                total = total + homebuf[other, source]
+            out_ref[source * 2 + 1] = unfold(total)
+
+    for h in range(PIECES):
+        to_core2(1, h).wait_send()
+    for d in partners:
+        to_home(d, z, t).wait_send()
+
+    @pl.when(z != home_of(1))
+    def _():
+        to_home(0, z, t).wait_send()
 
 
 def finish(sums_ref, out_hbm, both, sems):
@@ -475,24 +709,38 @@
             pltpu.VMEM((rows, LANES), f32),
             pltpu.VMEM((rows + HALF, points), bf16),
             pltpu.VMEM((2 * NT * QUARTERS * 4, NFFT), bf16),
-            pltpu.VMEM((QUARTERS, NT, pairs, 16, points), bf16),
-            pltpu.VMEM((QUARTERS, NT, pairs, 16, points), bf16),
+            pltpu.VMEM((FULL, NT, pairs, 16, points), bf16),
+            pltpu.VMEM((FULL, NT, pairs, 16, points), bf16),
+            pltpu.VMEM((NT, pairs // 2 + 1, 16, points), bf16),
+            pltpu.VMEM((NT, pairs // 2 + 1, 16, points), bf16),
+            pltpu.VMEM((NT, pairs // 2, 16, points), bf16),
+            pltpu.VMEM((NT, pairs // 2, 16, points), bf16),
             pltpu.VMEM((NFFT, points), bf16),
             pltpu.VMEM((NT, 2, 16, points), bf16),
             pltpu.VMEM((2, 16, points), bf16),
             pltpu.VMEM((points // LANES, 8 * SLOTS, LANES), f32),
-            pltpu.VMEM((QUARTERS, 2, 2, SLOTS, LANES), f32),
-            pltpu.VMEM((QUARTERS, 2, SLOTS, LANES), f32),
-            pltpu.VMEM((QUARTERS, 2, SLOTS, LANES), f32),
-            pltpu.VMEM((QUARTERS, NZ, SLOTS, LANES), f32),
-            pltpu.VMEM((NT, 2, SLOTS, LANES), f32),
+            pltpu.VMEM((FULL, 2, 2, KEPT, LANES), f32),
+            pltpu.VMEM((FULL, 2, KEPT, LANES), f32),
+            pltpu.VMEM((FULL, 2, KEPT, LANES), f32),
+            pltpu.VMEM((FULL, NZ, KEPT, LANES), f32),
+            pltpu.VMEM((2, 2, KEPT, LANES), f32),
+            pltpu.VMEM((2, KEPT, LANES), f32),
+            pltpu.VMEM((2, KEPT, LANES), f32),
+            pltpu.VMEM((NZ, KEPT, LANES), f32),
+            pltpu.VMEM((NZ, NT, KEPT, LANES), f32),
+            pltpu.VMEM((NT, 2, KEPT, LANES), f32),
             dma((6,)),
             dma, dma,
-            dma((QUARTERS, 3, NT - 1)), dma((QUARTERS, 3, NT - 1)),
+            dma((FULL, 3, NT - 1)), dma((FULL, 3, NT - 1)),
+            dma((NT - 1,)), dma((NT - 1,)),
+            dma((2, NT - 1)), dma((2, NT - 1)),
             dma((lane_tiles,)), dma((2, lane_tiles)),
             dma((lane_tiles, NT - 1)), dma((lane_tiles,)),
-            dma((QUARTERS, PIECES)), dma((QUARTERS, PIECES)),
-            dma((QUARTERS, 2, PIECES)), dma((QUARTERS, NZ, PIECES)),
+            dma((FULL, PIECES)), dma((FULL, PIECES)),
+            dma((FULL, 2, PIECES)), dma((FULL, NZ, PIECES)),
+            dma((2, PIECES)), dma((2, PIECES)),
+            dma((PIECES,)), dma((NZ, PIECES)),
+            dma((NT,)), dma((NZ, NT)),
             dma((2, PIECES, NT - 1)), dma((2, PIECES, NT - 1)),
         ],
         compiler_params=pltpu.CompilerParams(
@@ -552,7 +800,7 @@
             and np_ == 2 * NZ
             and freq_indices.shape[0] == 2 * nt * np_
             and points % LANES == 0
-            and rows % NFFT == HALF
+            and rows % (2 * NFFT) == NFFT + HALF
             and rows >= 16 * HOP
             and 4 * (rows // HOP) + 1 <= SLOTS
         )

time: 59.6 us -> 58.6 us (0.983)
  Pallas kernels: 59.5 us -> 58.5 us
    pallas_call x1, Pallas kernels: 58.5 us -> 57.5 us  [fused(): pl.pallas_call(functools.partial(kernel, total_points), out_shape=jax.Sha...]
where the time goes in v4:
time: 58.6 us; the launch traced here: 58.5 us
  Pallas kernels  58.5 us (100%)
    pallas_call x1, Pallas kernels, fused(): pl.pallas_call(functools.partial(kernel, total_points), out_shape=jax.Sha...  57.5 us

profile of v4, /device:TPU:8, one launch (start us, length us, event | category | flops | bytes accessed | tf_op | source)
XLA Modules:
  0.0 58.5 jit_solution(14236230833040006465)
XLA Ops:
  0.0 57.5 %spectra_cross.1.sums_ref = f32[8,96,128]{2,1,0:T(8,128)S(1)} custom-call(bf16[2880,640]{1,0:T(8,128)(2,1)} %codes_hbm.1, f32[2880]{0:T(1024)} %scales_hbm.1, f32[640]{0:T(1024)} %weights_hbm.1, s32[64]{0:T(128)} %freq_hbm.1), custom_call_target="tpu_custom_call" | custom-call | tf_op jit(solution)/shard_map/spectra_cross/pallas_call | solution.py:699
  57.5 1.0 %hermitian_parts.1 = f32[1424,89]{1,0:T(8,128)} custom-call(f32[8,96,128]{2,1,0:T(8,128)S(1)} %spectra_cross.1.sums_ref), custom_call_target="tpu_custom_call" | custom-call | tf_op jit(solution)/shard_map/hermitian_parts/pallas_call | solution.py:751

commit v5 on v4

--- a/solution.py
+++ b/solution.py
@@ -142,13 +142,6 @@
         cosine, sine = turn_waves(bins * sample % NFFT)
         return window_shape * jnp.where(sub % 2 == 0, cosine, -sine)
 
-    load_freq.wait()
-    for dest in range(NT):
-        for half in range(2):
-            at = dest * 32 + half * 16
-            pair = [octet_table(dest, 2 * half), octet_table(dest, 2 * half + 1)]
-            table[at:at + 16, :] = jnp.concatenate(pair, axis=0).astype(jnp.bfloat16)
-
     load_scales.wait()
     for g in range(-(-rows // HOP)):
         size = min(HOP, rows - g * HOP)
@@ -179,9 +172,6 @@
             send_sem=halo_s, recv_sem=halo_r,
             device_id=(t ^ 1, p), device_id_type=MESH,
         )
-
-    pl.semaphore_wait(barrier, NT + NZ - 1)
-    halo_copy(halo_to).start()
 
     load_early.wait()
     lax.fori_loop(early_at // HALF, (early_at + early) // HALF, dequantize, 0)
@@ -223,7 +213,7 @@
             sfirst[dest, quads] = mixed.astype(jnp.bfloat16)
 
     quads = pairs // 2
-    q_cut = 2
+    q_cut = 1
     cuts = (0, 2 * q_cut, pairs - 1, pairs)
     partners = (3, 1, 2)
 
@@ -248,7 +238,7 @@
             device_id=(t ^ d, p), device_id_type=MESH,
         )
 
-    last_cuts = (0, 3, quads)
+    last_cuts = (0, 4, quads)
 
     def exchange_last(piece, d, source):
         at = pl.ds(last_cuts[piece], last_cuts[piece + 1] - last_cuts[piece])
@@ -290,10 +280,20 @@
             exchange(q, piece, d, t).start()
 
 
+    pl.semaphore_wait(barrier, NT + NZ - 1)
+    halo_copy(halo_to).start()
+
     @pl.when(middle)
     def _():
         for lane in range(lane_tiles):
             hop_copy(lane, t, owner(lane)).start()
+
+    load_freq.wait()
+    for dest in range(NT):
+        for half in range(2):
+            at = dest * 32 + half * 16
+            pair = [octet_table(dest, 2 * half), octet_table(dest, 2 * half + 1)]
+            table[at:at + 16, :] = jnp.concatenate(pair, axis=0).astype(jnp.bfloat16)
 
     lax.fori_loop(0, q_cut, spectra, 0)
     send(0, 0)

time: 58.6 us -> 58.1 us (level)
  Pallas kernels: 58.5 us -> 57.9 us
where the time goes in v5:
time: 58.1 us; the launch traced here: 57.9 us
  Pallas kernels  57.9 us (100%)
    pallas_call x1, Pallas kernels, fused(): pl.pallas_call(functools.partial(kernel, total_points), out_shape=jax.Sha...  56.9 us

profile of v5, /device:TPU:8, one launch (start us, length us, event | category | flops | bytes accessed | tf_op | source)
XLA Modules:
  0.0 57.9 jit_solution(5954273088039012884)
XLA Ops:
  0.0 56.9 %spectra_cross.1.sums_ref = f32[8,96,128]{2,1,0:T(8,128)S(1)} custom-call(bf16[2880,640]{1,0:T(8,128)(2,1)} %codes_hbm.1, f32[2880]{0:T(1024)} %scales_hbm.1, f32[640]{0:T(1024)} %weights_hbm.1, s32[64]{0:T(128)} %freq_hbm.1), custom_call_target="tpu_custom_call" | custom-call | tf_op jit(solution)/shard_map/spectra_cross/pallas_call | solution.py:699
  56.9 1.0 %hermitian_parts.1 = f32[1424,89]{1,0:T(8,128)} custom-call(f32[8,96,128]{2,1,0:T(8,128)S(1)} %spectra_cross.1.sums_ref), custom_call_target="tpu_custom_call" | custom-call | tf_op jit(solution)/shard_map/hermitian_parts/pallas_call | solution.py:751

commit v6 on v5

--- a/solution.py
+++ b/solution.py
@@ -13,12 +13,13 @@
 HALF = HOP // 2
 LANES = 128
 SLOTS = 96
-KEPT = 72
+KEPT = 64
+SPAN = 89
 NT = 4
 NZ = 4
 QUARTERS = 4
 FULL = 3
-ROW_PARTS = ((0, 72),)
+ROW_PARTS = ((0, 64),)
 PIECES = len(ROW_PARTS)
 ZSETS = ((0, 3), (1, 2))
 ORDERS = (
@@ -59,24 +60,29 @@
 
 def fold(matrix):
     lane = lax.broadcasted_iota(jnp.int32, (KEPT, LANES), 1)
-    rest = jnp.zeros((LANES - (SLOTS - KEPT), LANES), jnp.float32)
+    size = SLOTS - KEPT
+    first = 2 * SPAN - KEPT
+    rest = jnp.zeros((LANES - size, LANES), jnp.float32)
     turned = jnp.concatenate([matrix[KEPT:], rest], axis=0).T
     corner = turned[KEPT:SLOTS]
-    corners = jnp.concatenate([pltpu.roll(corner, LANES - 8 * m, 1) for m in (1, 2, 3)], axis=0)
-    side = pltpu.roll(turned[:KEPT], SLOTS, 1)
-    return jnp.where(lane < SLOTS, matrix[:KEPT], jnp.where(lane < LANES - 8, side, corners))
+    corners = jnp.concatenate(
+        [pltpu.roll(corner, first, 1), pltpu.roll(corner, 2 * first - LANES, 1)], axis=0
+    )
+    side = pltpu.roll(turned[:KEPT], SPAN, 1)
+    return jnp.where(lane < SPAN, matrix[:KEPT], jnp.where(lane < first, side, corners))
 
 
 def unfold(folded):
     lane = lax.broadcasted_iota(jnp.int32, (KEPT, LANES), 1)
-    top = jnp.where(lane < SLOTS, folded, 0.0)
-    side = jnp.where(lane < SLOTS - KEPT, pltpu.roll(folded, LANES - SLOTS, 1), 0.0)
     size = SLOTS - KEPT
-    corner = jnp.zeros((size, LANES), jnp.float32)
-    for m in (1, 2, 3):
-        moved = pltpu.roll(folded[(m - 1) * size:m * size], 8 * m, 1)
-        here = lane[:size]
-        corner = jnp.where((here >= 8 * m - 8) & (here < 8 * m), moved, corner)
+    here = lane[:size]
+    wide = LANES - (2 * SPAN - KEPT)
+    top = jnp.where(lane < SPAN, folded, 0.0)
+    side = jnp.where(lane < SPAN - KEPT, pltpu.roll(folded, LANES - SPAN, 1), 0.0)
+    corner = jnp.where(
+        here < wide, pltpu.roll(folded[:size], wide, 1), pltpu.roll(folded[size:], 2 * wide, 1)
+    )
+    corner = jnp.where(here < SPAN - KEPT, corner, 0.0)
     rest = jnp.zeros((LANES - SLOTS, LANES), jnp.float32)
     turned = jnp.concatenate([side, corner, rest], axis=0).T
     return jnp.concatenate([top, turned[:size]], axis=0)
@@ -802,7 +808,7 @@
             and points % LANES == 0
             and rows % (2 * NFFT) == NFFT + HALF
             and rows >= 16 * HOP
-            and 4 * (rows // HOP) + 1 <= SLOTS
+            and NT * (rows // HOP) + 1 <= SPAN
         )
         if fits:
             return fused(codes, scales, weights, freq_indices, points * np_)

time: 58.1 us -> 57.7 us (level)
  no operation moved by 1% of the time
where the time goes in v6:
time: 57.7 us; the launch traced here: 57.6 us
  Pallas kernels  57.6 us (100%)
    pallas_call x1, Pallas kernels, fused(): pl.pallas_call(functools.partial(kernel, total_points), out_shape=jax.Sha...  56.6 us

profile of v6, /device:TPU:8, one launch (start us, length us, event | category | flops | bytes accessed | tf_op | source)
XLA Modules:
  0.0 57.6 jit_solution(6438302476127731358)
XLA Ops:
  0.0 56.6 %spectra_cross.1.sums_ref = f32[8,96,128]{2,1,0:T(8,128)S(1)} custom-call(bf16[2880,640]{1,0:T(8,128)(2,1)} %codes_hbm.1, f32[2880]{0:T(1024)} %scales_hbm.1, f32[640]{0:T(1024)} %weights_hbm.1, s32[64]{0:T(128)} %freq_hbm.1), custom_call_target="tpu_custom_call" | custom-call | tf_op jit(solution)/shard_map/spectra_cross/pallas_call | solution.py:705
  56.6 1.0 %hermitian_parts.1 = f32[1424,89]{1,0:T(8,128)} custom-call(f32[8,96,128]{2,1,0:T(8,128)S(1)} %spectra_cross.1.sums_ref), custom_call_target="tpu_custom_call" | custom-call | tf_op jit(solution)/shard_map/hermitian_parts/pallas_call | solution.py:757

commit v7 on v6

--- a/solution.py
+++ b/solution.py
@@ -724,7 +724,7 @@
             pltpu.VMEM((NFFT, points), bf16),
             pltpu.VMEM((NT, 2, 16, points), bf16),
             pltpu.VMEM((2, 16, points), bf16),
-            pltpu.VMEM((points // LANES, 8 * SLOTS, LANES), f32),
+            pltpu.VMEM((points // LANES, 12 * SLOTS, LANES), f32),
             pltpu.VMEM((FULL, 2, 2, KEPT, LANES), f32),
             pltpu.VMEM((FULL, 2, KEPT, LANES), f32),
             pltpu.VMEM((FULL, 2, KEPT, LANES), f32),
@@ -759,7 +759,7 @@
         out_shape=jax.ShapeDtypeStruct((2 * NT * 2 * count, count), f32),
         in_specs=[vmem],
         out_specs=hbm,
-        scratch_shapes=[pltpu.VMEM((2 * NT * 2 * count, count), f32), dma((2,))],
+        scratch_shapes=[pltpu.VMEM((2 * NT * 2 * count + 16, count), f32), dma((2,))],
         name="hermitian_parts",
     )(pltpu.with_memory_space_constraint(sums, pltpu.VMEM))
     return full.reshape(2 * NT, count, 2, count).transpose(0, 2, 1, 3)

time: 57.7 us -> 57.7 us (level)
  no operation moved by 1% of the time
where the time goes in v7:
time: 57.7 us; the launch traced here: 57.6 us
  Pallas kernels  57.6 us (100%)
    pallas_call x1, Pallas kernels, fused(): pl.pallas_call(functools.partial(kernel, total_points), out_shape=jax.Sha...  56.6 us

profile of v7, /device:TPU:8, one launch (start us, length us, event | category | flops | bytes accessed | tf_op | source)
XLA Modules:
  0.0 57.6 jit_solution(9674204613562253710)
XLA Ops:
  0.0 56.6 %spectra_cross.1.sums_ref = f32[8,96,128]{2,1,0:T(8,128)S(1)} custom-call(bf16[2880,640]{1,0:T(8,128)(2,1)} %codes_hbm.1, f32[2880]{0:T(1024)} %scales_hbm.1, f32[640]{0:T(1024)} %weights_hbm.1, s32[64]{0:T(128)} %freq_hbm.1), custom_call_target="tpu_custom_call" | custom-call | tf_op jit(solution)/shard_map/spectra_cross/pallas_call | solution.py:705
  56.6 1.0 %hermitian_parts.1 = f32[1424,89]{1,0:T(8,128)} custom-call(f32[8,96,128]{2,1,0:T(8,128)S(1)} %spectra_cross.1.sums_ref), custom_call_target="tpu_custom_call" | custom-call | tf_op jit(solution)/shard_map/hermitian_parts/pallas_call | solution.py:757
